TPU v7x, 32 devices: a whole 2x2x4 slice. The times are simulated.
32 devices in a mesh: seq: 8 (over y, x, core), head: 4 (over z).
Axes of the slice: x: 2, y: 2, z: 4, core: 2. Of those that a mesh axis runs over, the one named last changes fastest.
Arguments:
- row_queries: bfloat16 [8192, 2048], P('seq', 'head'), may hold values from -200 to 200
- row_keys: bfloat16 [8192, 2048], P('seq', 'head'), may hold values from -6 to 6
- row_values: bfloat16 [8192, 2048], P('seq', 'head'), may hold values from -6 to 6
- residual_in: bfloat16 [8192, 4096], P(('seq', 'head')), may hold values from -6 to 6
- out_weight: bfloat16 [2048, 4096], P('head', 'seq'), may hold values from -0.25 to 0.25
- norm_gain: float32 [4096], replicated, may hold values from 0.1 to 1.9
- qkv_weight: bfloat16 [4096, 16, 3, 128], P('seq', 'head'), may hold values from -4 to 4
Outputs:
- residual_out: bfloat16 [8192, 4096], P(('seq', 'head'))
- column_out: bfloat16 [8192, 2048], P('seq', 'head')
All inputs are finite; a program needn't handle non-finite values.
Results may differ from a plain program's by a relative error of at most 0.0091.
Values may be sent and summed in bfloat16 or wider, within the bound.
No kernel may reach another device: no remote copies, remote signals or barrier semaphores. Data moves between devices by JAX's collectives and lax.ppermute only.
A program may use at most 128 MiB of HBM per device.

v0:
```python
import jax
import jax.numpy as jnp
from jax import lax
from jax.sharding import PartitionSpec as P

HD = 128
COLS = 512


epsilon = 1e-05


def passed_along(array, axis, by):
    size = lax.axis_size(axis)
    pairs = [(i, i + by) for i in range(size) if 0 <= i + by < size]
    return lax.ppermute(array, axis, pairs)


def band_block(queries, keys, values, has_prev):
    width = queries.shape[0]
    scores = jnp.einsum("qhd,khd->hqk", queries, keys, preferred_element_type=jnp.float32) * HD ** (
        -0.5
    )
    query_col = jnp.arange(width, dtype=jnp.int32)[:, None]
    key_col = jnp.arange(2 * width, dtype=jnp.int32)[None, :]
    allowed = jnp.where(
        key_col < width, (key_col > query_col) & has_prev, key_col - width <= query_col
    )
    scores = jnp.where(allowed[None], scores, -jnp.inf)
    shifted = jnp.exp(scores - jnp.max(scores, -1, keepdims=True))
    weights = (shifted / jnp.sum(shifted, -1, keepdims=True)).astype(jnp.bfloat16)
    return jnp.einsum("hqk,khd->qhd", weights, values, preferred_element_type=jnp.float32).astype(
        jnp.bfloat16
    )


def normalize(stream_bf, norm_gain):
    stream = stream_bf.astype(jnp.float32)
    center = stream - jnp.mean(stream, -1, keepdims=True)
    variance = jnp.mean(center * center, -1, keepdims=True)
    return (center * lax.rsqrt(variance + epsilon) * norm_gain).astype(jnp.bfloat16)


def column_block(block):
    queries = block[..., :HD]
    keys = block[..., HD : 2 * HD]
    values = block[..., 2 * HD :]
    scores = jnp.einsum(
        "rchd,schd->chrs", queries, keys, preferred_element_type=jnp.float32
    ) * HD ** (-0.5)
    height = block.shape[0]
    allowed = (
        jnp.arange(height, dtype=jnp.int32)[None, :] <= jnp.arange(height, dtype=jnp.int32)[:, None]
    )
    scores = jnp.where(allowed[None, None], scores, -jnp.inf)
    shifted = jnp.exp(scores - jnp.max(scores, -1, keepdims=True))
    weights = (shifted / jnp.sum(shifted, -1, keepdims=True)).astype(jnp.bfloat16)
    return jnp.einsum(
        "chrs,schd->rchd", weights, values, preferred_element_type=jnp.float32
    ).astype(jnp.bfloat16)


def per_device(row_queries, row_keys, row_values, residual_in, out_weight, norm_gain, qkv_weight):
    positions = row_queries.shape[0]
    features = row_queries.shape[1]
    groups = features // HD
    slab_rows = positions // COLS
    key_back, value_back = passed_along((row_keys[-COLS:], row_values[-COLS:]), "seq", 1)
    all_keys = jnp.concatenate([key_back, row_keys], 0).reshape(-1, groups, HD)
    all_values = jnp.concatenate([value_back, row_values], 0).reshape(-1, groups, HD)
    first_row = lax.axis_index("seq") * slab_rows
    pieces = []
    for line in range(slab_rows):
        query_row = row_queries[line * COLS : (line + 1) * COLS].reshape(COLS, groups, HD)
        key_rows = all_keys[line * COLS : (line + 2) * COLS]
        value_rows = all_values[line * COLS : (line + 2) * COLS]
        pieces.append(
            band_block(query_row, key_rows, value_rows, first_row + line > 0).reshape(
                COLS, features
            )
        )
    row_out = jnp.concatenate(pieces, 0)
    full_out = lax.all_gather(out_weight, "seq", axis=1, tiled=True)
    share = residual_in.shape[0]
    offset = lax.axis_index("head") * share
    terms = jnp.dot(row_out, full_out, preferred_element_type=jnp.float32)
    own_terms = lax.dynamic_slice_in_dim(terms, offset, share, 0) + residual_in.astype(jnp.float32)
    terms = lax.dynamic_update_slice_in_dim(terms, own_terms, offset, 0)
    stream_all = lax.psum(terms, "head").astype(jnp.bfloat16)
    normed_all = normalize(stream_all, norm_gain)
    residual_out = lax.dynamic_slice_in_dim(stream_all, offset, share, 0)
    piece = lax.all_gather(qkv_weight, "seq", axis=0, tiled=True)
    flat = piece.reshape(piece.shape[0], -1)
    projected = jnp.dot(normed_all, flat, preferred_element_type=jnp.float32)
    column_qkv = projected.astype(jnp.bfloat16).reshape(slab_rows, COLS, groups, 3 * HD)
    attended = column_block(
        lax.all_to_all(column_qkv, "seq", split_axis=1, concat_axis=0, tiled=True)
    )
    restored = lax.all_to_all(attended, "seq", split_axis=0, concat_axis=1, tiled=True)
    return (residual_out, restored.reshape(positions, features))


def solution(mesh):
    placed = (
        P("seq", "head"),
        P("seq", "head"),
        P("seq", "head"),
        P(("seq", "head"), None),
        P("head", "seq"),
        P(),
        P("seq", "head", None, None),
    )
    return jax.shard_map(
        per_device,
        mesh=mesh,
        in_specs=placed,
        out_specs=(P(("seq", "head"), None), P("seq", "head")),
        check_vma=False,
    )
```

profile of v0, /device:TPU:0, one launch (start us, length us, event | category | flops | bytes accessed | tf_op | source)
XLA Modules:
  0.0 758.3 jit_solution(582884239480867547)
XLA Ops:
  10.3 3.1 collective-permute-start.1
  15.4 4.6 collective-permute-start
  19.9 3.8 copy.48
  29.4 2.3 fusion.34
  33.7 6.2 fusion.59
  39.9 5.1 fusion.32
  47.1 7.6 %fusion.60 = (f32[4,512]{1,0:T(4,128)S(1)}, f32[4,512,1024]{1,2,0:T(8,128)}) fusion(pred[512,1024]{0,1:T(8,128)(4,1)} %get-tuple-element.4, bf16[1024,4,128]{0,2,1:T(8,128)(2,1)S(1)} %bitcast.62, bf16[512,4,128]{0,2,1:T(8,128)(2,1)} %bitcast.64), kind=kOutput, calls=%fused_computation.81 | convolution fusion | flops 545260544 | bytes 10493952 | tf_op jit(solution)/shard_map/sub | solution.py:30
  56.4 4.2 fusion.33
  60.6 11.2 %fusion.41 = f32[1024,4096]{1,0:T(8,128)} fusion(bf16[512,4096]{1,0:T(8,128)(2,1)} %all-gather.3.cloned.1.call-done, bf16[512,512]{0,1:T(8,128)(2,1)S(1)} %bitcast.66, bf16[512,512]{0,1:T(8,128)(2,1)S(1)} %bitcast.67), kind=kOutput, calls=%fused_computation.57 | convolution fusion | flops 4297064448 | bytes 22020096 | tf_op jit(solution)/shard_map/dot_general | solution.py:86
  71.8 4.8 add_dynamic-update-slice_fusion
  76.7 558.8 %all-reduce.1 = bf16[1024,4096]{1,0:T(8,128)(2,1)} all-reduce(f32[1024,4096]{1,0:T(8,128)} %add_dynamic-update-slice_fusion), channel_id=1, replica_groups=mesh['seq'=8,'head'=4] {'head'}, use_global_device_ids=true, to_apply=%region_4.5 | all-reduce | flops 4194304 | bytes 25165824 | tf_op jit(solution)/shard_map/psum | solution.py:89
  635.4 4.7 convert_reduce_fusion
  641.2 2.3 fusion.5
  643.6 19.4 %fusion.23 = bf16[1024,1536]{1,0:T(8,128)(2,1)} fusion(bf16[4096,1536]{0,1:T(8,128)(2,1)} %bitcast.65, bf16[1024,4096]{1,0:T(8,128)(2,1)} %all-reduce.1, f32[4096]{0:T(1024)S(1)} %copy-done.6, f32[1024]{0:T(1024)S(1)} %add_rsqrt_fusion, f32[1024]{0:T(1024)S(1)} %broadcast_multiply_fusion), kind=kOutput, calls=%fused_computation.31 | convolution fusion | flops 12907446272 | bytes 24141824 | tf_op jit(solution)/shard_map/dot_general | solution.py:94
  662.9 5.0 reshape.169
  667.9 2.7 copy.49
  670.7 4.9 all-to-all-start
  675.5 37.9 %all-to-all-done = bf16[2,512,4,384]{3,2,0,1:T(4,128)(2,1)S(1)} async-done(((bf16[2,512,4,384]{3,2,0,1:T(4,128)(2,1)}), bf16[2,512,4,384]{3,2,0,1:T(4,128)(2,1)S(1)}, u32[]{:S(2)}, u32[]{:S(2)}) %all-to-all-start) | async-done | bytes 3145760 | tf_op jit(solution)/shard_map/all_to_all | solution.py:97
  713.4 5.2 copy.72
  718.6 6.4 all_to_all.27
  725.0 2.5 fusion.61
  731.0 3.6 all-to-all-start.1
  734.6 3.1 constant_dynamic-slice_fusion
  737.7 12.2 %all-to-all-done.1 = bf16[16,64,4,128]{3,2,1,0:T(4,128)(2,1)S(1)} async-done(((bf16[16,64,4,128]{3,2,1,0:T(4,128)(2,1)}), bf16[16,64,4,128]{3,2,1,0:T(4,128)(2,1)S(1)}, u32[]{:S(2)}, u32[]{:S(2)}) %all-to-all-start.1) | async-done | bytes 1048608 | tf_op jit(solution)/shard_map/all_to_all | solution.py:99
  (44 shorter events, 22.8 us)
Async XLA Ops:
  7.2 22.2 %copy-start.2 = (bf16[1024,512]{1,0:T(8,128)(2,1)S(1)}, bf16[1024,512]{1,0:T(8,128)(2,1)}, u32[]{:S(2)}) copy-start(bf16[1024,512]{1,0:T(8,128)(2,1)} %param.8) | copy-start | bytes 3145732
  7.2 16.6 %copy-start.1 = (bf16[1024,512]{1,0:T(8,128)(2,1)S(1)}, bf16[1024,512]{1,0:T(8,128)(2,1)}, u32[]{:S(2)}) copy-start(bf16[1024,512]{1,0:T(8,128)(2,1)} %param.9) | copy-start | bytes 3145732
  7.2 53.4 %all-gather.3.cloned.1.call-start = ((), (), s32[]{:S(2)}) async-start(), calls=%async_computation.2 | async-start | bytes 4718592 | tf_op jit(solution)/shard_map/all_gather | solution.py:83
  7.9 635.6 %all-gather.5.cloned.1.call-start = ((), (), s32[]{:S(2)}) async-start(), calls=%async_computation.3 | async-start | bytes 14155776 | tf_op jit(solution)/shard_map/all_gather | solution.py:92
  10.3 35.7 %collective-permute-start.1 = (bf16[512,512]{0,1:T(8,128)(2,1)}, bf16[512,512]{0,1:T(8,128)(2,1)}, u32[]{:S(2)}, u32[]{:S(2)}) collective-permute-start(bf16[512,512]{0,1:T(8,128)(2,1)} %slice.54), channel_id=1, source_target_pairs={{0,4},{4,8},{8,12},{12,16},{16,20},{20,24},{24,28},{1,5},{5,9},{9,... | collective-permute-start | bytes 1572872 | tf_op jit(solution)/shard_map/ppermute | solution.py:16
  15.4 39.4 %collective-permute-start = (bf16[512,512]{1,0:T(8,128)(2,1)}, bf16[512,512]{1,0:T(8,128)(2,1)}, u32[]{:S(2)}, u32[]{:S(2)}) collective-permute-start(bf16[512,512]{1,0:T(8,128)(2,1)} %slice.41), channel_id=1, source_target_pairs={{0,4},{4,8},{8,12},{12,16},{16,20},{20,24},{24,28},{1,5},{5,9},{9,... | collective-permute-start | bytes 1572872 | tf_op jit(solution)/shard_map/ppermute | solution.py:16
  33.7 6.2 copy-start.5
  39.9 5.1 copy-start.3
  56.4 4.2 copy-start.7
  60.6 11.2 %copy-start.4 = (bf16[256,4096]{1,0:T(8,128)(2,1)S(1)}, bf16[256,4096]{1,0:T(8,128)(2,1)}, u32[]{:S(2)}) copy-start(bf16[256,4096]{1,0:T(8,128)(2,1)} %param.10) | copy-start | bytes 6291460
  635.4 5.8 copy-start
  635.4 8.1 %copy-start.6 = (f32[4096]{0:T(1024)S(1)}, f32[4096]{0:T(1024)}, u32[]{:S(2)}) copy-start(f32[4096]{0:T(1024)} %param.12) | copy-start | bytes 49156
  670.7 42.7 %all-to-all-start = ((bf16[2,512,4,384]{3,2,0,1:T(4,128)(2,1)}), bf16[2,512,4,384]{3,2,0,1:T(4,128)(2,1)S(1)}, u32[]{:S(2)}, u32[]{:S(2)}) async-start(bf16[2,512,4,384]{3,2,0,1:T(4,128)(2,1)} %copy.49), calls=%async_computation | async-start | bytes 6291456 | tf_op jit(solution)/shard_map/all_to_all | solution.py:97
  731.0 18.9 %all-to-all-start.1 = ((bf16[16,64,4,128]{3,2,1,0:T(4,128)(2,1)}), bf16[16,64,4,128]{3,2,1,0:T(4,128)(2,1)S(1)}, u32[]{:S(2)}, u32[]{:S(2)}) async-start(bf16[16,64,4,128]{3,2,1,0:T(4,128)(2,1)} %copy.52), calls=%async_computation.1 | async-start | bytes 2097152 | tf_op jit(solution)/shard_map/all_to_all | solution.py:99
Sparse Core Ops, SparseCore 0:
  9.9 42.7 all-gather.2
  55.1 74.5 all-gather.4
where the time goes:
time: 759 us; the launch traced here: 758 us
  blocking collectives  559 us (74%)
  matrix products  54.3 us (7%)
  waiting for transfers between devices  50.8 us (7%)
  local copies, waits for them, and re-layouts  41.7 us (5%)
  other arithmetic  22.3 us (3%)
  starting transfers between devices  16.2 us (2%)
  between operations  14.2 us (2%)
    psum x1, blocking collectives, per_device(): stream_all = lax.psum(terms, 'head').astype(jnp.bfloat16)  559 us
    all_to_all x1, waiting for transfers between devices, per_device(): lax.all_to_all(column_qkv, 'seq', split_axis=1, concat_axis=0, tiled=True)  37.9 us
    dot_general x1, matrix products, per_device(): projected = jnp.dot(normed_all, flat, preferred_element_type=jnp.float32)  19.4 us
  transfers between devices with their start and end apart: 6, of which 2 were waited for; matrix products, arithmetic and copies ran while one was open for 9% of the time, Pallas kernels for 0%

commit v1 on v0

v1 whole, which is shorter than its diff:
```python
import functools

import jax
import jax.numpy as jnp
from jax import lax
from jax.experimental import pallas as pl
from jax.experimental.pallas import tpu as pltpu
from jax.sharding import PartitionSpec as P

HD = 128
COLS = 512
EPSILON = 1e-05
TILE = 256
EXP2_SCALE = HD ** (-0.5) * 1.4426950408889634
MASKED = -1e30
VMEM = 56 * 1024 * 1024


def params(grid_rank):
    return pltpu.CompilerParams(
        dimension_semantics=("arbitrary",) * grid_rank, vmem_limit_bytes=VMEM
    )


def softmax_values(scores, values):
    top = jnp.max(scores, -1, keepdims=True)
    shifted = jnp.exp2((scores - top) * EXP2_SCALE)
    total = jnp.sum(shifted, -1, keepdims=True)
    summed = jnp.dot(shifted.astype(jnp.bfloat16), values, preferred_element_type=jnp.float32)
    return (summed / total).astype(jnp.bfloat16)


def scores_of(queries, keys):
    return lax.dot_general(
        queries, keys, (((1,), (1,)), ((), ())), preferred_element_type=jnp.float32
    )


def band_kernel(first_ref, q_ref, kp_ref, kc_ref, vp_ref, vc_ref, o_ref):
    has_prev = first_ref[0] + pl.program_id(0) > 0
    for tile in range(COLS // TILE):
        low, high = tile * TILE, (tile + 1) * TILE
        queries = q_ref[low:high, :]
        keys = jnp.concatenate([kp_ref[low:, :], kc_ref[:high, :]], 0)
        values = jnp.concatenate([vp_ref[low:, :], vc_ref[:high, :]], 0)
        scores = scores_of(queries, keys)
        row = lax.broadcasted_iota(jnp.int32, scores.shape, 0)
        col = lax.broadcasted_iota(jnp.int32, scores.shape, 1)
        allowed = (col > row) & (col <= row + COLS) & ((col >= COLS - low) | has_prev)
        scores = jnp.where(allowed, scores, MASKED)
        o_ref[low:high, :] = softmax_values(scores, values)


def band_attention(first, queries, key_prev, key_now, value_prev, value_now, lines, q_at, prev_at, now_at):
    groups = queries.shape[1] // HD

    def block(at):
        return pl.BlockSpec((COLS, HD), lambda line, head, _: (line + at, head))

    return pl.pallas_call(
        band_kernel,
        grid_spec=pltpu.PrefetchScalarGridSpec(
            num_scalar_prefetch=1,
            grid=(lines, groups),
            in_specs=[block(q_at), block(prev_at), block(now_at), block(prev_at), block(now_at)],
            out_specs=block(0),
        ),
        out_shape=jax.ShapeDtypeStruct((lines * COLS, groups * HD), jnp.bfloat16),
        compiler_params=params(2),
        cost_estimate=pl.CostEstimate(
            flops=4 * lines * COLS * 768 * HD * groups,
            bytes_accessed=lines * COLS * groups * HD * 12,
            transcendentals=lines * COLS * 768 * groups,
        ),
        name="band_attention",
    )(first, queries, key_prev, key_now, value_prev, value_now)


def project_kernel(parts, width, *refs):
    row_refs, (own_ref, far_ref, residual_ref, gain_ref, out_ref, normed_ref) = (
        refs[:parts],
        refs[parts:],
    )
    step = pl.program_id(0)
    terms = residual_ref[...].astype(jnp.float32)
    for part in range(parts):
        weight = own_ref[0] if part == 0 else far_ref[0, part - 1]
        terms += jnp.dot(row_refs[part][...], weight, preferred_element_type=jnp.float32)
    out_ref[:, pl.ds(pl.multiple_of(step * width, width), width)] = terms.astype(jnp.bfloat16)

    @pl.when(step == pl.num_programs(0) - 1)
    def _():
        rows = out_ref.shape[0]
        tile = min(rows, 64)

        def norm(at, _):
            here = pl.ds(pl.multiple_of(at * tile, tile), tile)
            stream = out_ref[here, :].astype(jnp.float32)
            center = stream - jnp.mean(stream, -1, keepdims=True)
            variance = jnp.mean(center * center, -1, keepdims=True)
            normed_ref[here, :] = (
                center * lax.rsqrt(variance + EPSILON) * gain_ref[...]
            ).astype(jnp.bfloat16)
            return 0

        lax.fori_loop(0, rows // tile, norm, 0)


def project_and_norm(row_parts, own_weight, far_weight, residual, gain):
    steps, depth, width = own_weight.shape
    parts = len(row_parts)
    rows, features = residual.shape
    whole = pl.BlockSpec((rows, features), lambda i: (0, 0))
    return pl.pallas_call(
        functools.partial(project_kernel, parts, width),
        grid=(steps,),
        in_specs=[pl.BlockSpec((rows, depth), lambda i: (0, 0))] * parts
        + [
            pl.BlockSpec((1, depth, width), lambda i: (i, 0, 0)),
            pl.BlockSpec((1, parts - 1, depth, width), lambda i: (i, 0, 0, 0)),
            pl.BlockSpec((rows, width), lambda i: (0, i)),
            pl.BlockSpec((1, features), lambda i: (0, 0)),
        ],
        out_specs=[whole, whole],
        out_shape=[jax.ShapeDtypeStruct((rows, features), jnp.bfloat16)] * 2,
        compiler_params=params(1),
        cost_estimate=pl.CostEstimate(
            flops=2 * rows * parts * depth * features,
            bytes_accessed=2 * parts * own_weight.size + 6 * rows * features,
            transcendentals=rows,
        ),
        name="project_and_norm",
    )(*row_parts, own_weight, far_weight, residual, gain)


def column_kernel(columns, qkv_ref, o_ref):
    height = qkv_ref.shape[0] // columns
    part = min(qkv_ref.shape[0], 256)
    for low in range(0, height * columns, part):
        high = low + part
        scores = scores_of(qkv_ref[low:high, :HD], qkv_ref[:high, HD : 2 * HD])
        row = lax.broadcasted_iota(jnp.int32, scores.shape, 0) + low
        col = lax.broadcasted_iota(jnp.int32, scores.shape, 1)
        allowed = (col <= row) & (((row - col) & (columns - 1)) == 0)
        scores = jnp.where(allowed, scores, MASKED)
        o_ref[low:high] = softmax_values(scores, qkv_ref[:high, 2 * HD :])


def column_attention(qkv):
    height, columns, features = qkv.shape
    groups = features // (3 * HD)
    attended = pl.pallas_call(
        functools.partial(column_kernel, columns),
        grid=(groups,),
        in_specs=[pl.BlockSpec((height * columns, 3 * HD), lambda g: (0, g))],
        out_specs=pl.BlockSpec((height * columns, HD), lambda g: (0, g)),
        out_shape=jax.ShapeDtypeStruct((height * columns, groups * HD), jnp.bfloat16),
        compiler_params=params(1),
        cost_estimate=pl.CostEstimate(
            flops=4 * height * columns * groups * 256 * HD,
            bytes_accessed=8 * height * columns * groups * HD,
            transcendentals=height * columns * groups * 256,
        ),
        name="column_attention",
    )(qkv.reshape(height * columns, features))
    return attended.reshape(height, columns, groups * HD)


def passed_along(array, axis, by):
    size = lax.axis_size(axis)
    pairs = [(i, i + by) for i in range(size) if 0 <= i + by < size]
    return lax.ppermute(array, axis, pairs)


def moved(value, pairs):
    return lax.ppermute(value, "head", pairs)


def line_first(array):
    return moved(array, [(0, 1), (1, 2), (2, 3)]), moved(array, [(1, 0), (2, 1), (3, 2)])


def line_second(array, below, above):
    place = lax.axis_index("head")
    at_end = (place == 0) | (place == 3)
    below_two = moved(below, [(1, 2), (2, 3)])
    above_two = moved(above, [(2, 1), (1, 0)])
    across = moved(array, [(0, 3), (3, 0)])
    slots = [
        (below, (place + 3) % 4),
        (above, (place + 1) % 4),
        (jnp.where(place < 2, above_two, below_two), (place + 2) % 4),
        (jnp.where(at_end, across, array), jnp.where(at_end, 3 - place, place)),
    ]
    gathered = lax.dynamic_update_index_in_dim(
        jnp.zeros((4, *array.shape), array.dtype), array, place, 0
    )
    for value, slot in slots:
        gathered = lax.dynamic_update_index_in_dim(gathered, value, slot, 0)
    return gathered


def from_behind(array, by):
    size = lax.axis_size("head")
    return moved(array, [(i, (i + by) % size) for i in range(size)])


def after(value, *others):
    return lax.optimization_barrier((value, *others))[0]


def per_device(row_queries, row_keys, row_values, residual_in, out_weight, norm_gain, qkv_weight):
    positions, features = row_queries.shape
    lines = positions // COLS
    seq, heads = lax.axis_size("seq"), lax.axis_size("head")
    place = lax.axis_index("head")
    share, model = residual_in.shape
    gain = norm_gain.reshape(1, model)
    block = min(share, COLS)
    blocks = COLS // block
    quarter = share // 4
    late = 3

    own_weight = lax.all_gather(out_weight, "seq")
    far_weight = [from_behind(out_weight, by) for by in range(1, heads)]
    key_back, value_back = passed_along((row_keys[-COLS:], row_values[-COLS:]), "seq", 1)
    residual = residual_in.reshape(share // block, 4, block // 4, model)
    residual_own = residual[:, 0].reshape(quarter, model)
    residual_first = jnp.stack([residual_own] * heads)
    for by in range(1, heads):
        residual_first = lax.dynamic_update_index_in_dim(
            residual_first, from_behind(residual_own, by), (place + heads - by) % heads, 0
        )
    residual_first = residual_first.reshape(heads * quarter, model)

    first_row = (lax.axis_index("seq") * lines).reshape(1)
    row_out = []
    if lines > 1:
        row_out.append(
            band_attention(
                first_row + 1,
                row_queries,
                row_keys,
                row_keys,
                row_values,
                row_values,
                lines - 1,
                1,
                0,
                1,
            )
        )
    row_out.insert(
        0,
        band_attention(
            first_row, row_queries, key_back, row_keys, value_back, row_values, 1, 0, 0, 0
        ),
    )
    row_out = jnp.concatenate(row_out, 0)
    far_weight = lax.all_gather(after(jnp.stack(far_weight), row_out), "seq")

    row_out = row_out.reshape(heads, share // block, 4, block // 4, features)
    row_first = row_out[:, :, 0].reshape(heads * quarter, features)
    row_late = row_out[:, :, 1:].reshape(heads, late * quarter, features)
    parts_first = [row_first] + [from_behind(row_first, by) for by in range(1, heads)]
    parts_late = [
        from_behind(
            lax.dynamic_index_in_dim(row_late, (place + by) % heads, 0, keepdims=False), by
        )
        if by
        else lax.dynamic_index_in_dim(row_late, place, 0, keepdims=False)
        for by in range(heads)
    ]
    qkv_own = after(qkv_weight.reshape(qkv_weight.shape[0], -1), *parts_late)
    qkv_flat = lax.all_gather(qkv_own, "seq", axis=0, tiled=True)

    out_late, normed_own = project_and_norm(
        parts_late, own_weight, far_weight, residual[:, 1:].reshape(late * quarter, model), gain
    )
    normed_own = normed_own.reshape(share // block, late, block // 4, model)
    normed_own = [normed_own[:, low:high].reshape(-1, model) for low, high in ((0, 2), (2, 3))]
    copies = [line_first(piece) for piece in normed_own]
    out_first, normed_first = project_and_norm(
        parts_first, own_weight, far_weight, residual_first, gain
    )
    out_first = lax.dynamic_slice_in_dim(out_first, place * quarter, quarter, 0)
    normed = [
        line_second(piece, *first).reshape(-1, model) for piece, first in zip(normed_own, copies)
    ]
    normed.insert(0, after(normed_first, normed[0], *copies[1]))

    def project(normed):
        own_columns = normed.shape[0] // (lines * seq)
        projected = jnp.dot(normed, qkv_flat, preferred_element_type=jnp.float32)
        qkv = projected.astype(jnp.bfloat16).reshape(lines, seq, own_columns, -1)
        return qkv.transpose(1, 0, 2, 3)

    def swap(pieces):
        return lax.all_to_all(pieces, "seq", split_axis=0, concat_axis=0, tiled=True)

    def attend(qkv):
        return column_attention(qkv.reshape(seq * lines, *qkv.shape[2:]))

    def send_back(attended):
        own_columns = attended.shape[1]
        attended = swap(attended.reshape(seq, lines, own_columns, features))
        return attended.transpose(1, 0, 2, 3).reshape(
            lines, blocks, seq * own_columns // blocks, features
        )

    qkv_first = swap(project(normed[0]))
    qkv_next = project(normed[1])
    qkv_end = project(after(normed[2], qkv_first, qkv_next))
    qkv_next = swap(qkv_next)
    sent = [send_back(attend(qkv_first))]
    qkv_end = swap(after(qkv_end, qkv_next, *sent))
    sent += [send_back(attend(qkv_next)), send_back(attend(qkv_end))]
    column_out = jnp.concatenate(sent, 2)
    residual_out = jnp.concatenate(
        [
            out_first.reshape(share // block, 1, block // 4, model),
            out_late.reshape(share // block, late, block // 4, model),
        ],
        1,
    )
    return residual_out.reshape(share, model), column_out.reshape(positions, features)


def solution(mesh):
    placed = (
        P("seq", "head"),
        P("seq", "head"),
        P("seq", "head"),
        P(("seq", "head"), None),
        P("head", "seq"),
        P(),
        P("seq", "head", None, None),
    )
    return jax.shard_map(
        per_device,
        mesh=mesh,
        in_specs=placed,
        out_specs=(P(("seq", "head"), None), P("seq", "head")),
        check_vma=False,
    )
```

time: 759 us -> 397 us (0.52)
  blocking collectives: 559 us -> 0 us
  waiting for transfers between devices: 50.8 us -> 174 us
  starting transfers between devices: 16.2 us -> 85.4 us
  Pallas kernels: 0 us -> 54.7 us
  matrix products: 54.3 us -> 28.3 us
  local copies, waits for them, and re-layouts: 41.7 us -> 27.4 us
  other arithmetic: 22.3 us -> 11.1 us
    psum x1 -> x0, blocking collectives: 559 us -> none  [per_device(): stream_all = lax.psum(terms, 'head').astype(jnp.bfloat16)]
    ppermute x0 -> x22, waiting for transfers between devices: none -> 127 us  [moved(): return lax.ppermute(value, 'head', pairs)]
    ppermute x0 -> x22, starting transfers between devices: none -> 56.8 us  [moved(): return lax.ppermute(value, 'head', pairs)]
    pallas_call x0 -> x7, Pallas kernels: none -> 54.7 us  [the longest x2 29.2 us: project_and_norm(): pl.pallas_call(functools.partial(project_kernel, parts, width), grid=(ste...]
    dot_general x6 -> x3, matrix products: 44.2 us -> 28.3 us  [project(): projected = jnp.dot(normed, qkv_flat, preferred_element_type=jnp.float32)]
    all_to_all x2 -> x6, waiting for transfers between devices: 50.1 us -> 36.9 us  [swap(): lax.all_to_all(pieces, 'seq', split_axis=0, concat_axis=0, tiled=True)]
    all_to_all x2 -> x6, starting transfers between devices: 8.42 us -> 21.5 us  [swap(): lax.all_to_all(pieces, 'seq', split_axis=0, concat_axis=0, tiled=True)]
    all_to_all x3, local copies, waits for them, and re-layouts: 11.9 us -> 0.08 us  [swap(): lax.all_to_all(pieces, 'seq', split_axis=0, concat_axis=0, tiled=True)]
  transfers between devices with their start and end apart: 6 -> 33, of which waited for: 2 -> 13; matrix products, arithmetic and copies ran while one was open for 9% -> 15% of each run, Pallas kernels for 0% -> 14%
where the time goes in v1:
time: 397 us; the launch traced here: 396 us
  waiting for transfers between devices  174 us (44%)
  starting transfers between devices  85.4 us (22%)
  Pallas kernels  54.7 us (14%)
  matrix products  28.3 us (7%)
  local copies, waits for them, and re-layouts  27.4 us (7%)
  between operations  14.3 us (4%)
  other arithmetic  11.1 us (3%)
    ppermute x22, waiting for transfers between devices, moved(): return lax.ppermute(value, 'head', pairs)  127 us
    ppermute x22, starting transfers between devices, moved(): return lax.ppermute(value, 'head', pairs)  56.8 us
    all_to_all x6, waiting for transfers between devices, swap(): lax.all_to_all(pieces, 'seq', split_axis=0, concat_axis=0, tiled=True)  36.9 us
    pallas_call x2, Pallas kernels, project_and_norm(): pl.pallas_call(functools.partial(project_kernel, parts, width), grid=(ste...  29.2 us
    dot_general x3, matrix products, project(): projected = jnp.dot(normed, qkv_flat, preferred_element_type=jnp.float32)  28.3 us
    all_to_all x6, starting transfers between devices, swap(): lax.all_to_all(pieces, 'seq', split_axis=0, concat_axis=0, tiled=True)  21.5 us
    pallas_call x3, Pallas kernels, column_attention(): pl.pallas_call(functools.partial(column_kernel, columns), grid=(groups,),...  13.1 us
    pallas_call x2, Pallas kernels, band_attention(): pl.pallas_call(band_kernel, grid_spec=pltpu.PrefetchScalarGridSpec(num_sc...  12.4 us
  transfers between devices with their start and end apart: 33, of which 13 were waited for; matrix products, arithmetic and copies ran while one was open for 15% of the time, Pallas kernels for 14%

profile of v1, /device:TPU:0, one launch (start us, length us, event | category | flops | bytes accessed | tf_op | source)
XLA Modules:
  0.0 395.6 jit_solution(6748088999674730842)
XLA Ops:
  12.5 4.5 %collective-permute-start.1 = (bf16[512,512]{1,0:T(8,128)(2,1)S(1)}, bf16[512,512]{1,0:T(8,128)(2,1)S(1)}, u32[]{:S(2)}, u32[]{:S(2)}) collective-permute-start(bf16[512,512]{1,0:T(8,128)(2,1)S(1)} %slice.25), channel_id=1, source_target_pairs={{0,4},{4,8},{8,12},{12,16},{16,20},{20,24},{24,28},{1,5},{5,9},{9,... | collective-permute-start | bytes 1572872 | tf_op jit(solution)/shard_map/ppermute | solution.py:172
  21.7 6.2 %band_attention.3 = bf16[512,512]{1,0:T(8,128)(2,1)} custom-call(s32[1]{0:T(128)S(6)} %add.76.first_ref, bf16[1024,512]{1,0:T(8,128)(2,1)} %q_ref.3, bf16[1024,512]{1,0:T(8,128)(2,1)} %kc_ref.3, bf16[1024,512]{1,0:T(8,128)(2,1)} %kc_ref.3, bf16[1024,512]{1,0:T(8,128)(2,1)} %vc_ref.3, bf16[1024,512]{1,0:T(8,128)(2,1)} %vc_ref.3), custom_call_target="tpu_custom_call" | custom-call | flops 805306368 | bytes 3145728 | tf_op jit(solution)/shard_map/band_attention/pallas_call | solution.py:60
  29.5 6.2 %band_attention.2 = bf16[512,512]{1,0:T(8,128)(2,1)} custom-call(s32[1]{0:T(128)} %bitcast.first_ref, bf16[1024,512]{1,0:T(8,128)(2,1)} %q_ref.3, bf16[512,512]{1,0:T(8,128)(2,1)} %copy-done.9, bf16[1024,512]{1,0:T(8,128)(2,1)} %kc_ref.3, bf16[512,512]{1,0:T(8,128)(2,1)} %copy-done.10, bf16[1024,512]{1,0:T(8,128)(2,1)} %vc_ref.3), custom_call_target="tpu_custom_call" | custom-call | flops 805306368 | bytes 3145728 | tf_op jit(solution)/shard_map/band_attention/pallas_call | solution.py:60
  36.8 28.9 %collective-permute-done.6 = bf16[512,512]{1,0:T(8,128)(2,1)} collective-permute-done((bf16[512,512]{1,0:T(8,128)(2,1)S(1)}, bf16[512,512]{1,0:T(8,128)(2,1)}, u32[]{:S(2)}, u32[]{:S(2)}) %collective-permute-start.6) | collective-permute-done | bytes 524320 | tf_op jit(solution)/shard_map/ppermute | solution.py:176
  79.2 6.6 %collective-permute-done.12.refs_2_ = bf16[192,512]{1,0:T(8,128)(2,1)S(1)} collective-permute-done((bf16[192,512]{1,0:T(8,128)(2,1)}, bf16[192,512]{1,0:T(8,128)(2,1)S(1)}, u32[]{:S(2)}, u32[]{:S(2)}) %collective-permute-start.12) | collective-permute-done | bytes 196640 | tf_op jit(solution)/shard_map/ppermute | solution.py:176
  87.1 4.3 %collective-permute-start.8 = (bf16[64,4096]{1,0:T(8,128)(2,1)S(1)}, bf16[64,4096]{1,0:T(8,128)(2,1)S(1)}, u32[]{:S(2)}, u32[]{:S(2)}) collective-permute-start(bf16[64,4096]{1,0:T(8,128)(2,1)S(1)} %slice_bitcast_fusion), channel_id=1, source_target_pairs={{0,1},{1,2},{2,3},{3,0},{4,5},{5,6},{6,7},{7,4},{8,9},{9,10},{10,1... | collective-permute-start | bytes 1572872 | tf_op jit(solution)/shard_map/ppermute | solution.py:176
  99.2 7.0 %collective-permute-done.8 = bf16[64,4096]{1,0:T(8,128)(2,1)S(1)} collective-permute-done((bf16[64,4096]{1,0:T(8,128)(2,1)S(1)}, bf16[64,4096]{1,0:T(8,128)(2,1)S(1)}, u32[]{:S(2)}, u32[]{:S(2)}) %collective-permute-start.8) | collective-permute-done | bytes 524320 | tf_op jit(solution)/shard_map/ppermute | solution.py:176
  111.2 17.6 %collective-permute-done.9 = bf16[64,4096]{1,0:T(8,128)(2,1)} collective-permute-done((bf16[64,4096]{1,0:T(8,128)(2,1)S(1)}, bf16[64,4096]{1,0:T(8,128)(2,1)}, u32[]{:S(2)}, u32[]{:S(2)}) %collective-permute-start.9) | collective-permute-done | bytes 524320 | tf_op jit(solution)/shard_map/ppermute | solution.py:176
  130.0 10.1 %all-gather.10.cloned.1.call-done = bf16[24,512,512]{2,1,0:T(8,128)(2,1)} async-done(((bf16[3,512,512]{2,1,0:T(8,128)(2,1)}), bf16[24,512,512]{2,1,0:T(8,128)(2,1)}) %all-gather.10.cloned.1.call-update) | async-done | bytes 12582928 | tf_op jit(solution)/shard_map/all_gather | solution.py:260
  140.1 13.9 %project_and_norm.3 = (bf16[192,4096]{1,0:T(8,128)(2,1)}, bf16[192,4096]{1,0:T(8,128)(2,1)}) custom-call(bf16[192,512]{1,0:T(8,128)(2,1)} %get-tuple-element.23.refs_0_, bf16[192,512]{1,0:T(8,128)(2,1)} %copy-done.14, bf16[192,512]{1,0:T(8,128)(2,1)} %copy-done.15, bf16[192,512]{1,0:T(8,128)(2,1)} %copy-done.16, bf16[8,512,512]{2,1,0:T(8,128)(2,1)} %bitcast.99, ...), custom_call_target="tpu_custom_call" | custom-call | flops 3221225472 | bytes 21495808 | tf_op jit(solution)/shard_map/project_and_norm/pallas_call | solution.py:114
  155.2 12.8 %collective-permute-start.19 = (bf16[64,4096]{1,0:T(8,128)(2,1)S(1)}, bf16[64,4096]{1,0:T(8,128)(2,1)S(1)}, u32[]{:S(2)}, u32[]{:S(2)}) collective-permute-start(bf16[64,4096]{1,0:T(8,128)(2,1)S(1)} %slice_bitcast_fusion.1), channel_id=1, source_target_pairs={{0,1},{1,2},{2,3},{4,5},{5,6},{6,7},{8,9},{9,10},{10,11},{12,13},{... | collective-permute-start | bytes 1572872 | tf_op jit(solution)/shard_map/ppermute | solution.py:176
  171.8 7.2 %collective-permute-start.23 = (bf16[64,4096]{1,0:T(8,128)(2,1)S(1)}, bf16[64,4096]{1,0:T(8,128)(2,1)S(1)}, u32[]{:S(2)}, u32[]{:S(2)}) collective-permute-start(bf16[64,4096]{1,0:T(8,128)(2,1)S(1)} %slice_bitcast_fusion.1), channel_id=1, source_target_pairs={{0,3},{3,0},{4,7},{7,4},{8,11},{11,8},{12,15},{15,12},{16,19},{19,... | collective-permute-start | bytes 1572872 | tf_op jit(solution)/shard_map/ppermute | solution.py:176
  181.8 15.3 %project_and_norm.2 = (bf16[256,4096]{1,0:T(8,128)(2,1)}, bf16[256,4096]{1,0:T(8,128)(2,1)}) custom-call(bf16[256,512]{1,0:T(8,128)(2,1)} %bitcast.130, bf16[256,512]{1,0:T(8,128)(2,1)} %collective-permute-done.2.refs_1_, bf16[256,512]{1,0:T(8,128)(2,1)} %collective-permute-done.3.refs_2_, bf16[256,512]{1,0:T(8,128)(2,1)} %collective-permute-done.4.refs_3_, ...), custom_call_target="tpu_custom_call" | custom-call | flops 4294967296 | bytes 23068672 | tf_op jit(solution)/shard_map/project_and_norm/pallas_call | solution.py:114
  197.7 5.2 %collective-permute-start.18 = (bf16[128,4096]{1,0:T(8,128)(2,1)S(1)}, bf16[128,4096]{1,0:T(8,128)(2,1)S(1)}, u32[]{:S(2)}, u32[]{:S(2)}) collective-permute-start(bf16[128,4096]{1,0:T(8,128)(2,1)S(1)} %bitcast.104), channel_id=1, source_target_pairs={{0,3},{3,0},{4,7},{7,4},{8,11},{11,8},{12,15},{15,12},{16,19},{19,... | collective-permute-start | bytes 3145736 | tf_op jit(solution)/shard_map/ppermute | solution.py:176
  205.9 13.8 %collective-permute-done.15 = bf16[128,4096]{1,0:T(8,128)(2,1)S(1)} collective-permute-done((bf16[128,4096]{1,0:T(8,128)(2,1)S(1)}, bf16[128,4096]{1,0:T(8,128)(2,1)S(1)}, u32[]{:S(2)}, u32[]{:S(2)}) %collective-permute-start.15) | collective-permute-done | bytes 1048608 | tf_op jit(solution)/shard_map/ppermute | solution.py:176
  222.0 51.0 %collective-permute-done.16 = bf16[128,4096]{1,0:T(8,128)(2,1)S(1)} collective-permute-done((bf16[128,4096]{1,0:T(8,128)(2,1)S(1)}, bf16[128,4096]{1,0:T(8,128)(2,1)S(1)}, u32[]{:S(2)}, u32[]{:S(2)}) %collective-permute-start.16) | collective-permute-done | bytes 1048608 | tf_op jit(solution)/shard_map/ppermute | solution.py:176
  277.1 8.7 %convolution_convert_fusion.2 = bf16[256,1536]{1,0:T(8,128)(2,1)S(1)} fusion(bf16[256,4096]{1,0:T(8,128)(2,1)} %get-tuple-element.16, bf16[4096,1536]{0,1:T(8,128)(2,1)} %all-gather.6.cloned.1.call-done), kind=kOutput, calls=%fused_computation.2 | convolution fusion | flops 3221618688 | bytes 15466496 | tf_op jit(solution)/shard_map/dot_general | solution.py:294
  291.3 11.5 %all-to-all-done = bf16[8,2,16,1536]{3,2,1,0:T(8,128)(2,1)S(1)} async-done(((bf16[8,2,16,1536]{3,2,1,0:T(8,128)(2,1)}), bf16[8,2,16,1536]{3,2,1,0:T(8,128)(2,1)S(1)}, u32[]{:S(2)}, u32[]{:S(2)}) %all-to-all-start) | async-done | bytes 786464 | tf_op jit(solution)/shard_map/all_to_all | solution.py:299
  311.1 11.0 %convolution_convert_fusion = bf16[512,1536]{1,0:T(8,128)(2,1)S(1)} fusion(bf16[512,4096]{1,0:T(8,128)(2,1)} %bitcast.116, bf16[4096,1536]{0,1:T(8,128)(2,1)} %all-gather.6.cloned.1.call-done), kind=kOutput, calls=%fused_computation | convolution fusion | flops 6443237376 | bytes 18350080 | tf_op jit(solution)/shard_map/dot_general | solution.py:294
  329.4 8.6 %convolution_convert_fusion.1 = bf16[256,1536]{1,0:T(8,128)(2,1)S(1)} fusion(bf16[256,4096]{1,0:T(8,128)(2,1)} %bitcast.51, bf16[4096,1536]{0,1:T(8,128)(2,1)} %all-gather.6.cloned.1.call-done), kind=kOutput, calls=%fused_computation.1 | convolution fusion | flops 3221618688 | bytes 15466496 | tf_op jit(solution)/shard_map/dot_general | solution.py:294
  339.0 9.4 %all-to-all-done.2 = bf16[8,2,32,1536]{3,2,1,0:T(8,128)(2,1)S(1)} async-done(((bf16[8,2,32,1536]{3,2,1,0:T(8,128)(2,1)}), bf16[8,2,32,1536]{3,2,1,0:T(8,128)(2,1)S(1)}, u32[]{:S(2)}, u32[]{:S(2)}) %all-to-all-start.2) | async-done | bytes 1572896 | tf_op jit(solution)/shard_map/all_to_all | solution.py:299
  352.0 5.1 %column_attention.4 = bf16[512,512]{1,0:T(8,128)(2,1)} custom-call(bf16[512,1536]{1,0:T(8,128)(2,1)} %bitcast.108), custom_call_target="tpu_custom_call" | custom-call | flops 268435456 | bytes 2097152 | tf_op jit(solution)/shard_map/column_attention/pallas_call | solution.py:152
  357.1 7.4 %all-to-all-done.4 = bf16[8,2,16,1536]{3,2,1,0:T(8,128)(2,1)S(1)} async-done(((bf16[8,2,16,1536]{3,2,1,0:T(8,128)(2,1)}), bf16[8,2,16,1536]{3,2,1,0:T(8,128)(2,1)S(1)}, u32[]{:S(2)}, u32[]{:S(2)}) %all-to-all-start.4) | async-done | bytes 786464 | tf_op jit(solution)/shard_map/all_to_all | solution.py:299
  373.2 4.6 %all-to-all-done.3 = bf16[8,2,32,512]{3,2,1,0:T(8,128)(2,1)S(1)} async-done(((bf16[8,2,32,512]{3,2,1,0:T(8,128)(2,1)}), bf16[8,2,32,512]{3,2,1,0:T(8,128)(2,1)S(1)}, u32[]{:S(2)}, u32[]{:S(2)}) %all-to-all-start.3) | async-done | bytes 524320 | tf_op jit(solution)/shard_map/all_to_all | solution.py:299
  (126 shorter events, 104.2 us)
Async XLA Ops:
  7.2 122.8 %all-gather.8.cloned.1.call-start = ((), (), s32[]{:S(2)}) async-start(), calls=%async_computation.7 | async-start | bytes 4718592 | tf_op jit(solution)/shard_map/all_gather | solution.py:224
  7.9 132.2 %all-gather.10.cloned.1.call-start = ((), (), s32[]{:S(2)}) async-start(), calls=%async_computation.8 | async-start | bytes 14155776 | tf_op jit(solution)/shard_map/all_gather | solution.py:260
  9.0 18.9 %collective-permute-start = (bf16[512,512]{1,0:T(8,128)(2,1)S(1)}, bf16[512,512]{1,0:T(8,128)(2,1)S(1)}, u32[]{:S(2)}, u32[]{:S(2)}) collective-permute-start(bf16[512,512]{1,0:T(8,128)(2,1)S(1)} %slice.24), channel_id=1, source_target_pairs={{0,4},{4,8},{8,12},{12,16},{16,20},{20,24},{24,28},{1,5},{5,9},{9,... | collective-permute-start | bytes 1572872 | tf_op jit(solution)/shard_map/ppermute | solution.py:172
  17.0 19.8 %collective-permute-start.7 = (bf16[512,512]{1,0:T(8,128)(2,1)S(1)}, bf16[512,512]{1,0:T(8,128)(2,1)S(1)}, u32[]{:S(2)}, u32[]{:S(2)}) collective-permute-start(bf16[512,512]{1,0:T(8,128)(2,1)S(1)} %copy-done.11), channel_id=1, source_target_pairs={{0,3},{1,0},{2,1},{3,2},{4,7},{5,4},{6,5},{7,6},{8,11},{9,8},{10,9... | collective-permute-start | bytes 1572872 | tf_op jit(solution)/shard_map/ppermute | solution.py:176
  20.7 45.0 %collective-permute-start.6 = (bf16[512,512]{1,0:T(8,128)(2,1)S(1)}, bf16[512,512]{1,0:T(8,128)(2,1)}, u32[]{:S(2)}, u32[]{:S(2)}) collective-permute-start(bf16[512,512]{1,0:T(8,128)(2,1)S(1)} %copy-done.11), channel_id=1, source_target_pairs={{0,2},{1,3},{2,0},{3,1},{4,6},{5,7},{6,4},{7,5},{8,10},{9,11},{10,... | collective-permute-start | bytes 1572872 | tf_op jit(solution)/shard_map/ppermute | solution.py:176
  20.7 45.0 %collective-permute-start.5 = (bf16[512,512]{1,0:T(8,128)(2,1)S(1)}, bf16[512,512]{1,0:T(8,128)(2,1)}, u32[]{:S(2)}, u32[]{:S(2)}) collective-permute-start(bf16[512,512]{1,0:T(8,128)(2,1)S(1)} %copy-done.11), channel_id=1, source_target_pairs={{0,1},{1,2},{2,3},{3,0},{4,5},{5,6},{6,7},{7,4},{8,9},{9,10},{10,1... | collective-permute-start | bytes 1572872 | tf_op jit(solution)/shard_map/ppermute | solution.py:176
  68.3 208.9 %all-gather.6.cloned.1.call-start = ((), (), s32[]{:S(2)}) async-start(), calls=%async_computation.6 | async-start | bytes 14155776 | tf_op jit(solution)/shard_map/all_gather | solution.py:275
  87.1 19.1 %collective-permute-start.8 = (bf16[64,4096]{1,0:T(8,128)(2,1)S(1)}, bf16[64,4096]{1,0:T(8,128)(2,1)S(1)}, u32[]{:S(2)}, u32[]{:S(2)}) collective-permute-start(bf16[64,4096]{1,0:T(8,128)(2,1)S(1)} %slice_bitcast_fusion), channel_id=1, source_target_pairs={{0,1},{1,2},{2,3},{3,0},{4,5},{5,6},{6,7},{7,4},{8,9},{9,10},{10,1... | collective-permute-start | bytes 1572872 | tf_op jit(solution)/shard_map/ppermute | solution.py:176
  91.4 37.4 %collective-permute-start.9 = (bf16[64,4096]{1,0:T(8,128)(2,1)S(1)}, bf16[64,4096]{1,0:T(8,128)(2,1)}, u32[]{:S(2)}, u32[]{:S(2)}) collective-permute-start(bf16[64,4096]{1,0:T(8,128)(2,1)S(1)} %slice_bitcast_fusion), channel_id=1, source_target_pairs={{0,2},{1,3},{2,0},{3,1},{4,6},{5,7},{6,4},{7,5},{8,10},{9,11},{10,... | collective-permute-start | bytes 1572872 | tf_op jit(solution)/shard_map/ppermute | solution.py:176
  93.8 36.1 %collective-permute-start.10 = (bf16[64,4096]{1,0:T(8,128)(2,1)S(1)}, bf16[64,4096]{1,0:T(8,128)(2,1)S(1)}, u32[]{:S(2)}, u32[]{:S(2)}) collective-permute-start(bf16[64,4096]{1,0:T(8,128)(2,1)S(1)} %slice_bitcast_fusion), channel_id=1, source_target_pairs={{0,3},{1,0},{2,1},{3,2},{4,7},{5,4},{6,5},{7,6},{8,11},{9,8},{10,9... | collective-permute-start | bytes 1572872 | tf_op jit(solution)/shard_map/ppermute | solution.py:176
  96.6 75.2 %collective-permute-start.2 = (bf16[256,512]{1,0:T(8,128)(2,1)S(1)}, bf16[256,512]{1,0:T(8,128)(2,1)}, u32[]{:S(2)}, u32[]{:S(2)}) collective-permute-start(bf16[256,512]{1,0:T(8,128)(2,1)S(1)} %bitcast.127), channel_id=1, source_target_pairs={{0,1},{1,2},{2,3},{3,0},{4,5},{5,6},{6,7},{7,4},{8,9},{9,10},{10,1... | collective-permute-start | bytes 786440 | tf_op jit(solution)/shard_map/ppermute | solution.py:176
  98.6 80.5 %collective-permute-start.3 = (bf16[256,512]{1,0:T(8,128)(2,1)S(1)}, bf16[256,512]{1,0:T(8,128)(2,1)}, u32[]{:S(2)}, u32[]{:S(2)}) collective-permute-start(bf16[256,512]{1,0:T(8,128)(2,1)S(1)} %bitcast.128), channel_id=1, source_target_pairs={{0,2},{1,3},{2,0},{3,1},{4,6},{5,7},{6,4},{7,5},{8,10},{9,11},{10,... | collective-permute-start | bytes 786440 | tf_op jit(solution)/shard_map/ppermute | solution.py:176
  107.0 73.5 %collective-permute-start.4 = (bf16[256,512]{1,0:T(8,128)(2,1)S(1)}, bf16[256,512]{1,0:T(8,128)(2,1)}, u32[]{:S(2)}, u32[]{:S(2)}) collective-permute-start(bf16[256,512]{1,0:T(8,128)(2,1)S(1)} %bitcast.129), channel_id=1, source_target_pairs={{0,3},{1,0},{2,1},{3,2},{4,7},{5,4},{6,5},{7,6},{8,11},{9,8},{10,9... | collective-permute-start | bytes 786440 | tf_op jit(solution)/shard_map/ppermute | solution.py:176
  155.2 42.5 %collective-permute-start.19 = (bf16[64,4096]{1,0:T(8,128)(2,1)S(1)}, bf16[64,4096]{1,0:T(8,128)(2,1)S(1)}, u32[]{:S(2)}, u32[]{:S(2)}) collective-permute-start(bf16[64,4096]{1,0:T(8,128)(2,1)S(1)} %slice_bitcast_fusion.1), channel_id=1, source_target_pairs={{0,1},{1,2},{2,3},{4,5},{5,6},{6,7},{8,9},{9,10},{10,11},{12,13},{... | collective-permute-start | bytes 1572872 | tf_op jit(solution)/shard_map/ppermute | solution.py:176
  168.1 34.8 %collective-permute-start.20 = (bf16[64,4096]{1,0:T(8,128)(2,1)S(1)}, bf16[64,4096]{1,0:T(8,128)(2,1)S(1)}, u32[]{:S(2)}, u32[]{:S(2)}) collective-permute-start(bf16[64,4096]{1,0:T(8,128)(2,1)S(1)} %slice_bitcast_fusion.1), channel_id=1, source_target_pairs={{1,0},{2,1},{3,2},{5,4},{6,5},{7,6},{9,8},{10,9},{11,10},{13,12},{... | collective-permute-start | bytes 1572872 | tf_op jit(solution)/shard_map/ppermute | solution.py:176
  171.8 155.6 %collective-permute-start.23 = (bf16[64,4096]{1,0:T(8,128)(2,1)S(1)}, bf16[64,4096]{1,0:T(8,128)(2,1)S(1)}, u32[]{:S(2)}, u32[]{:S(2)}) collective-permute-start(bf16[64,4096]{1,0:T(8,128)(2,1)S(1)} %slice_bitcast_fusion.1), channel_id=1, source_target_pairs={{0,3},{3,0},{4,7},{7,4},{8,11},{11,8},{12,15},{15,12},{16,19},{19,... | collective-permute-start | bytes 1572872 | tf_op jit(solution)/shard_map/ppermute | solution.py:176
  179.1 41.9 %collective-permute-start.14 = (bf16[128,4096]{1,0:T(8,128)(2,1)S(1)}, bf16[128,4096]{1,0:T(8,128)(2,1)S(1)}, u32[]{:S(2)}, u32[]{:S(2)}) collective-permute-start(bf16[128,4096]{1,0:T(8,128)(2,1)S(1)} %bitcast.101), channel_id=1, source_target_pairs={{0,1},{1,2},{2,3},{4,5},{5,6},{6,7},{8,9},{9,10},{10,11},{12,13},{... | collective-permute-start | bytes 3145736 | tf_op jit(solution)/shard_map/ppermute | solution.py:176
  180.5 39.2 %collective-permute-start.15 = (bf16[128,4096]{1,0:T(8,128)(2,1)S(1)}, bf16[128,4096]{1,0:T(8,128)(2,1)S(1)}, u32[]{:S(2)}, u32[]{:S(2)}) collective-permute-start(bf16[128,4096]{1,0:T(8,128)(2,1)S(1)} %bitcast.102), channel_id=1, source_target_pairs={{1,0},{2,1},{3,2},{5,4},{6,5},{7,6},{9,8},{10,9},{11,10},{13,12},{... | collective-permute-start | bytes 3145736 | tf_op jit(solution)/shard_map/ppermute | solution.py:176
  197.7 77.2 %collective-permute-start.18 = (bf16[128,4096]{1,0:T(8,128)(2,1)S(1)}, bf16[128,4096]{1,0:T(8,128)(2,1)S(1)}, u32[]{:S(2)}, u32[]{:S(2)}) collective-permute-start(bf16[128,4096]{1,0:T(8,128)(2,1)S(1)} %bitcast.104), channel_id=1, source_target_pairs={{0,3},{3,0},{4,7},{7,4},{8,11},{11,8},{12,15},{15,12},{16,19},{19,... | collective-permute-start | bytes 3145736 | tf_op jit(solution)/shard_map/ppermute | solution.py:176
  202.9 87.4 %collective-permute-start.21 = (bf16[64,4096]{1,0:T(8,128)(2,1)S(1)}, bf16[64,4096]{1,0:T(8,128)(2,1)S(1)}, u32[]{:S(2)}, u32[]{:S(2)}) collective-permute-start(bf16[64,4096]{1,0:T(8,128)(2,1)S(1)} %collective-permute-done.20), channel_id=1, source_target_pairs={{2,1},{1,0},{6,5},{5,4},{10,9},{9,8},{14,13},{13,12},{18,17},{17,1... | collective-permute-start | bytes 1572872 | tf_op jit(solution)/shard_map/ppermute | solution.py:176
  219.7 53.3 %collective-permute-start.16 = (bf16[128,4096]{1,0:T(8,128)(2,1)S(1)}, bf16[128,4096]{1,0:T(8,128)(2,1)S(1)}, u32[]{:S(2)}, u32[]{:S(2)}) collective-permute-start(bf16[128,4096]{1,0:T(8,128)(2,1)S(1)} %collective-permute-done.15), channel_id=1, source_target_pairs={{2,1},{1,0},{6,5},{5,4},{10,9},{9,8},{14,13},{13,12},{18,17},{17,1... | collective-permute-start | bytes 3145736 | tf_op jit(solution)/shard_map/ppermute | solution.py:176
  221.0 53.5 %collective-permute-start.17 = (bf16[128,4096]{1,0:T(8,128)(2,1)S(1)}, bf16[128,4096]{1,0:T(8,128)(2,1)S(1)}, u32[]{:S(2)}, u32[]{:S(2)}) collective-permute-start(bf16[128,4096]{1,0:T(8,128)(2,1)S(1)} %collective-permute-done.14), channel_id=1, source_target_pairs={{1,2},{2,3},{5,6},{6,7},{9,10},{10,11},{13,14},{14,15},{17,18},{18... | collective-permute-start | bytes 3145736 | tf_op jit(solution)/shard_map/ppermute | solution.py:176
  273.1 17.2 %collective-permute-start.22 = (bf16[64,4096]{1,0:T(8,128)(2,1)S(1)}, bf16[64,4096]{1,0:T(8,128)(2,1)}, u32[]{:S(2)}, u32[]{:S(2)}) collective-permute-start(bf16[64,4096]{1,0:T(8,128)(2,1)S(1)} %collective-permute-done.19), channel_id=1, source_target_pairs={{1,2},{2,3},{5,6},{6,7},{9,10},{10,11},{13,14},{14,15},{17,18},{18... | collective-permute-start | bytes 1572872 | tf_op jit(solution)/shard_map/ppermute | solution.py:176
  323.3 25.1 %all-to-all-start.2 = ((bf16[8,2,32,1536]{3,2,1,0:T(8,128)(2,1)}), bf16[8,2,32,1536]{3,2,1,0:T(8,128)(2,1)S(1)}, u32[]{:S(2)}, u32[]{:S(2)}) async-start(bf16[8,2,32,1536]{3,2,1,0:T(8,128)(2,1)} %bitcast.94), calls=%async_computation.2 | async-start | bytes 3145728 | tf_op jit(solution)/shard_map/all_to_all | solution.py:299
  (26 other events, 267.7 us)
Sparse Core Ops, SparseCore 0:
  9.9 42.0 all-gather.7
  68.4 71.6 all-gather.9
  142.0 74.5 all-gather.5

commit v2 on v1

--- a/solution.py
+++ b/solution.py
@@ -172,20 +172,32 @@
     return lax.ppermute(array, axis, pairs)
 
 
+def from_behind(array, by):
+    size = lax.axis_size("head")
+    return lax.ppermute(array, "head", [(i, (i + by) % size) for i in range(size)])
+
+
+def after(value, *others):
+    return lax.optimization_barrier((value, *others))[0]
+
+
 def moved(value, pairs):
     return lax.ppermute(value, "head", pairs)
 
 
 def line_first(array):
-    return moved(array, [(0, 1), (1, 2), (2, 3)]), moved(array, [(1, 0), (2, 1), (3, 2)])
-
-
-def line_second(array, below, above):
+    return (
+        moved(array, [(0, 1), (1, 2), (2, 3)]),
+        moved(array, [(1, 0), (2, 1), (3, 2)]),
+        moved(array, [(0, 3), (3, 0)]),
+    )
+
+
+def line_second(array, below, above, across):
     place = lax.axis_index("head")
     at_end = (place == 0) | (place == 3)
     below_two = moved(below, [(1, 2), (2, 3)])
     above_two = moved(above, [(2, 1), (1, 0)])
-    across = moved(array, [(0, 3), (3, 0)])
     slots = [
         (below, (place + 3) % 4),
         (above, (place + 1) % 4),
@@ -198,15 +210,6 @@
     for value, slot in slots:
         gathered = lax.dynamic_update_index_in_dim(gathered, value, slot, 0)
     return gathered
-
-
-def from_behind(array, by):
-    size = lax.axis_size("head")
-    return moved(array, [(i, (i + by) % size) for i in range(size)])
-
-
-def after(value, *others):
-    return lax.optimization_barrier((value, *others))[0]
 
 
 def per_device(row_queries, row_keys, row_values, residual_in, out_weight, norm_gain, qkv_weight):
@@ -218,23 +221,22 @@
     gain = norm_gain.reshape(1, model)
     block = min(share, COLS)
     blocks = COLS // block
-    quarter = share // 4
-    late = 3
+    half = share // 2
 
     own_weight = lax.all_gather(out_weight, "seq")
-    far_weight = [from_behind(out_weight, by) for by in range(1, heads)]
+    far_weight = jnp.stack([from_behind(out_weight, by) for by in range(1, heads)])
+
     key_back, value_back = passed_along((row_keys[-COLS:], row_values[-COLS:]), "seq", 1)
-    residual = residual_in.reshape(share // block, 4, block // 4, model)
-    residual_own = residual[:, 0].reshape(quarter, model)
-    residual_first = jnp.stack([residual_own] * heads)
-    for by in range(1, heads):
-        residual_first = lax.dynamic_update_index_in_dim(
-            residual_first, from_behind(residual_own, by), (place + heads - by) % heads, 0
-        )
-    residual_first = residual_first.reshape(heads * quarter, model)
+    halves = residual_in.reshape(share // block, 2, block // 2, model)
+    residual_own = halves[:, 0].reshape(half, model)
+    residual_first = line_second(residual_own, *line_first(residual_own))
 
     first_row = (lax.axis_index("seq") * lines).reshape(1)
-    row_out = []
+    row_out = [
+        band_attention(
+            first_row, row_queries, key_back, row_keys, value_back, row_values, 1, 0, 0, 0
+        )
+    ]
     if lines > 1:
         row_out.append(
             band_attention(
@@ -250,78 +252,62 @@
                 1,
             )
         )
-    row_out.insert(
-        0,
-        band_attention(
-            first_row, row_queries, key_back, row_keys, value_back, row_values, 1, 0, 0, 0
-        ),
-    )
     row_out = jnp.concatenate(row_out, 0)
-    far_weight = lax.all_gather(after(jnp.stack(far_weight), row_out), "seq")
-
-    row_out = row_out.reshape(heads, share // block, 4, block // 4, features)
-    row_first = row_out[:, :, 0].reshape(heads * quarter, features)
-    row_late = row_out[:, :, 1:].reshape(heads, late * quarter, features)
+    far_weight = after(far_weight, row_out)
+    qkv_own = after(qkv_weight.reshape(qkv_weight.shape[0], -1), far_weight)
+    far_weight = lax.all_gather(far_weight, "seq")
+    qkv_flat = lax.all_gather(qkv_own, "seq", axis=0, tiled=True)
+    row_out = row_out.reshape(heads, share // block, 2, block // 2, features)
+    row_first = row_out[:, :, 0].reshape(heads * half, features)
+    row_last = row_out[:, :, 1].reshape(heads, half, features)
+
     parts_first = [row_first] + [from_behind(row_first, by) for by in range(1, heads)]
-    parts_late = [
+    parts_last = [
         from_behind(
-            lax.dynamic_index_in_dim(row_late, (place + by) % heads, 0, keepdims=False), by
+            lax.dynamic_index_in_dim(row_last, (place + by) % heads, 0, keepdims=False), by
         )
         if by
-        else lax.dynamic_index_in_dim(row_late, place, 0, keepdims=False)
+        else lax.dynamic_index_in_dim(row_last, place, 0, keepdims=False)
         for by in range(heads)
     ]
-    qkv_own = after(qkv_weight.reshape(qkv_weight.shape[0], -1), *parts_late)
-    qkv_flat = lax.all_gather(qkv_own, "seq", axis=0, tiled=True)
-
-    out_late, normed_own = project_and_norm(
-        parts_late, own_weight, far_weight, residual[:, 1:].reshape(late * quarter, model), gain
-    )
-    normed_own = normed_own.reshape(share // block, late, block // 4, model)
-    normed_own = [normed_own[:, low:high].reshape(-1, model) for low, high in ((0, 2), (2, 3))]
-    copies = [line_first(piece) for piece in normed_own]
+    out_last, normed_last = project_and_norm(
+        parts_last, own_weight, far_weight, halves[:, 1].reshape(half, model), gain
+    )
     out_first, normed_first = project_and_norm(
-        parts_first, own_weight, far_weight, residual_first, gain
-    )
-    out_first = lax.dynamic_slice_in_dim(out_first, place * quarter, quarter, 0)
-    normed = [
-        line_second(piece, *first).reshape(-1, model) for piece, first in zip(normed_own, copies)
-    ]
-    normed.insert(0, after(normed_first, normed[0], *copies[1]))
-
-    def project(normed):
-        own_columns = normed.shape[0] // (lines * seq)
+        parts_first, own_weight, far_weight, residual_first.reshape(heads * half, model), gain
+    )
+    out_first = lax.dynamic_slice_in_dim(out_first, place * half, half, 0)
+    copies = line_first(normed_last)
+    normed_first = after(normed_first, *copies[:2])
+    normed_last = line_second(normed_last, *copies).reshape(heads * half, model)
+
+    def attend(normed):
+        own_columns = COLS // 2 // seq
         projected = jnp.dot(normed, qkv_flat, preferred_element_type=jnp.float32)
         qkv = projected.astype(jnp.bfloat16).reshape(lines, seq, own_columns, -1)
-        return qkv.transpose(1, 0, 2, 3)
-
-    def swap(pieces):
-        return lax.all_to_all(pieces, "seq", split_axis=0, concat_axis=0, tiled=True)
-
-    def attend(qkv):
-        return column_attention(qkv.reshape(seq * lines, *qkv.shape[2:]))
+        qkv = lax.all_to_all(
+            qkv.transpose(1, 0, 2, 3), "seq", split_axis=0, concat_axis=0, tiled=True
+        )
+        return column_attention(qkv.reshape(seq * lines, own_columns, -1))
 
     def send_back(attended):
         own_columns = attended.shape[1]
-        attended = swap(attended.reshape(seq, lines, own_columns, features))
-        return attended.transpose(1, 0, 2, 3).reshape(
-            lines, blocks, seq * own_columns // blocks, features
-        )
-
-    qkv_first = swap(project(normed[0]))
-    qkv_next = project(normed[1])
-    qkv_end = project(after(normed[2], qkv_first, qkv_next))
-    qkv_next = swap(qkv_next)
-    sent = [send_back(attend(qkv_first))]
-    qkv_end = swap(after(qkv_end, qkv_next, *sent))
-    sent += [send_back(attend(qkv_next)), send_back(attend(qkv_end))]
-    column_out = jnp.concatenate(sent, 2)
-    residual_out = jnp.concatenate(
-        [
-            out_first.reshape(share // block, 1, block // 4, model),
-            out_late.reshape(share // block, late, block // 4, model),
-        ],
-        1,
+        attended = lax.all_to_all(
+            attended.reshape(seq, lines, own_columns, features),
+            "seq",
+            split_axis=0,
+            concat_axis=0,
+            tiled=True,
+        )
+        return attended.transpose(1, 0, 2, 3).reshape(lines, blocks, block // 2, features)
+
+    attended_first = attend(normed_first)
+    sent_first = send_back(attended_first)
+    attended_last = attend(after(normed_last, attended_first))
+    sent_last = send_back(after(attended_last, sent_first))
+    column_out = jnp.stack([sent_first, sent_last], 2)
+    residual_out = jnp.stack(
+        [piece.reshape(share // block, block // 2, model) for piece in (out_first, out_last)], 1
     )
     return residual_out.reshape(share, model), column_out.reshape(positions, features)
 

time: 397 us -> 391 us (0.985)
  matrix products: 28.3 us -> 21.9 us
  starting transfers between devices: 85.4 us -> 80.1 us
    ppermute x0 -> x9, waiting for transfers between devices: none -> 29.1 us  [from_behind(): lax.ppermute(array, 'head', [(i, (i + by) % size) for i in range(size)])]
    ppermute x0 -> x9, starting transfers between devices: none -> 22.4 us  [from_behind(): lax.ppermute(array, 'head', [(i, (i + by) % size) for i in range(size)])]
    ppermute x22 -> x10, starting transfers between devices: 56.8 us -> 36.2 us  [moved(): return lax.ppermute(value, 'head', pairs)]
    all_to_all x6 -> x4, waiting for transfers between devices: 36.9 us -> 26.2 us  [the longest x2 16 us: attend(): lax.all_to_all(qkv.transpose(1, 0, 2, 3), 'seq', split_axis=0, concat_axi...]
    all_gather x1, waiting for transfers between devices: 10.1 us -> 0.02 us  [per_device(): far_weight = lax.all_gather(far_weight, 'seq')]
    ppermute x22 -> x10, waiting for transfers between devices: 127 us -> 119 us  [moved(): return lax.ppermute(value, 'head', pairs)]
    all_to_all x6 -> x4, starting transfers between devices: 21.5 us -> 14.4 us  [the longest x2 7.46 us: attend(): lax.all_to_all(qkv.transpose(1, 0, 2, 3), 'seq', split_axis=0, concat_axi...]
    dot_general x3 -> x2, matrix products: 28.3 us -> 21.9 us  [attend(): projected = jnp.dot(normed, qkv_flat, preferred_element_type=jnp.float32)]
  transfers between devices with their start and end apart: 33 -> 28, of which waited for: 13 -> 10; matrix products, arithmetic and copies ran while one was open for 15% -> 15% of each run, Pallas kernels for 14% -> 14%
where the time goes in v2:
time: 391 us; the launch traced here: 390 us
  waiting for transfers between devices  175 us (45%)
  starting transfers between devices  80.1 us (20%)
  Pallas kernels  55.8 us (14%)
  local copies, waits for them, and re-layouts  30.5 us (8%)
  matrix products  21.9 us (6%)
  between operations  14.2 us (4%)
  other arithmetic  12.4 us (3%)
    ppermute x10, waiting for transfers between devices, moved(): return lax.ppermute(value, 'head', pairs)  119 us
    ppermute x10, starting transfers between devices, moved(): return lax.ppermute(value, 'head', pairs)  36.2 us
    pallas_call x2, Pallas kernels, project_and_norm(): pl.pallas_call(functools.partial(project_kernel, parts, width), grid=(ste...  33.3 us
    ppermute x9, waiting for transfers between devices, from_behind(): lax.ppermute(array, 'head', [(i, (i + by) % size) for i in range(size)])  29.1 us
    ppermute x9, starting transfers between devices, from_behind(): lax.ppermute(array, 'head', [(i, (i + by) % size) for i in range(size)])  22.4 us
    dot_general x2, matrix products, attend(): projected = jnp.dot(normed, qkv_flat, preferred_element_type=jnp.float32)  21.9 us
    all_to_all x2, waiting for transfers between devices, attend(): lax.all_to_all(qkv.transpose(1, 0, 2, 3), 'seq', split_axis=0, concat_axi...  16 us
    pallas_call x2, Pallas kernels, band_attention(): pl.pallas_call(band_kernel, grid_spec=pltpu.PrefetchScalarGridSpec(num_sc...  12.4 us
  transfers between devices with their start and end apart: 28, of which 10 were waited for; matrix products, arithmetic and copies ran while one was open for 15% of the time, Pallas kernels for 14%

profile of v2, /device:TPU:0, one launch (start us, length us, event | category | flops | bytes accessed | tf_op | source)
XLA Modules:
  0.0 389.7 jit_solution(9936467676084960370)
XLA Ops:
  12.5 4.5 %collective-permute-start.1 = (bf16[512,512]{1,0:T(8,128)(2,1)S(1)}, bf16[512,512]{1,0:T(8,128)(2,1)S(1)}, u32[]{:S(2)}, u32[]{:S(2)}) collective-permute-start(bf16[512,512]{1,0:T(8,128)(2,1)S(1)} %slice.19), channel_id=1, source_target_pairs={{0,4},{4,8},{8,12},{12,16},{16,20},{20,24},{24,28},{1,5},{5,9},{9,... | collective-permute-start | bytes 1572872 | tf_op jit(solution)/shard_map/ppermute | solution.py:172
  22.6 6.2 %band_attention.3 = bf16[512,512]{1,0:T(8,128)(2,1)} custom-call(s32[1]{0:T(128)S(6)} %add.63.first_ref, bf16[1024,512]{1,0:T(8,128)(2,1)} %q_ref.3, bf16[1024,512]{1,0:T(8,128)(2,1)} %kc_ref.3, bf16[1024,512]{1,0:T(8,128)(2,1)} %kc_ref.3, bf16[1024,512]{1,0:T(8,128)(2,1)} %vc_ref.3, bf16[1024,512]{1,0:T(8,128)(2,1)} %vc_ref.3), custom_call_target="tpu_custom_call" | custom-call | flops 805306368 | bytes 3145728 | tf_op jit(solution)/shard_map/band_attention/pallas_call | solution.py:60
  30.4 6.2 %band_attention.2 = bf16[512,512]{1,0:T(8,128)(2,1)} custom-call(s32[1]{0:T(128)} %bitcast.first_ref, bf16[1024,512]{1,0:T(8,128)(2,1)} %q_ref.3, bf16[512,512]{1,0:T(8,128)(2,1)} %copy-done.6, bf16[1024,512]{1,0:T(8,128)(2,1)} %kc_ref.3, bf16[512,512]{1,0:T(8,128)(2,1)} %copy-done.7, bf16[1024,512]{1,0:T(8,128)(2,1)} %vc_ref.3), custom_call_target="tpu_custom_call" | custom-call | flops 805306368 | bytes 3145728 | tf_op jit(solution)/shard_map/band_attention/pallas_call | solution.py:60
  37.9 17.8 %collective-permute-done.6 = bf16[512,512]{1,0:T(8,128)(2,1)} collective-permute-done((bf16[512,512]{1,0:T(8,128)(2,1)}, bf16[512,512]{1,0:T(8,128)(2,1)}, u32[]{:S(2)}, u32[]{:S(2)}) %collective-permute-start.6) | collective-permute-done | bytes 524320 | tf_op jit(solution)/shard_map/ppermute | solution.py:177
  58.6 3.7 copy.31
  63.8 14.6 %collective-permute-start.8 = (bf16[128,4096]{1,0:T(8,128)(2,1)}, bf16[128,4096]{1,0:T(8,128)(2,1)}, u32[]{:S(2)}, u32[]{:S(2)}) collective-permute-start(bf16[128,4096]{1,0:T(8,128)(2,1)} %get-tuple-element.16), channel_id=1, source_target_pairs={{0,1},{1,2},{2,3},{4,5},{5,6},{6,7},{8,9},{9,10},{10,11},{12,13},{... | collective-permute-start | bytes 3145736 | tf_op jit(solution)/shard_map/ppermute | solution.py:185
  79.7 5.6 %collective-permute-start.12 = (bf16[128,4096]{1,0:T(8,128)(2,1)}, bf16[128,4096]{1,0:T(8,128)(2,1)}, u32[]{:S(2)}, u32[]{:S(2)}) collective-permute-start(bf16[128,4096]{1,0:T(8,128)(2,1)} %get-tuple-element.16), channel_id=1, source_target_pairs={{0,3},{3,0},{4,7},{7,4},{8,11},{11,8},{12,15},{15,12},{16,19},{19,... | collective-permute-start | bytes 3145736 | tf_op jit(solution)/shard_map/ppermute | solution.py:185
  88.2 51.0 %collective-permute-done.9 = bf16[128,4096]{1,0:T(8,128)(2,1)} collective-permute-done((bf16[128,4096]{1,0:T(8,128)(2,1)}, bf16[128,4096]{1,0:T(8,128)(2,1)}, u32[]{:S(2)}, u32[]{:S(2)}) %collective-permute-start.9) | collective-permute-done | bytes 1048608 | tf_op jit(solution)/shard_map/ppermute | solution.py:185
  144.0 30.4 %collective-permute-done.10 = bf16[128,4096]{1,0:T(8,128)(2,1)S(1)} collective-permute-done((bf16[128,4096]{1,0:T(8,128)(2,1)}, bf16[128,4096]{1,0:T(8,128)(2,1)S(1)}, u32[]{:S(2)}, u32[]{:S(2)}) %collective-permute-start.10) | collective-permute-done | bytes 1048608 | tf_op jit(solution)/shard_map/ppermute | solution.py:185
  174.4 16.1 %collective-permute-start.13 = (bf16[128,512]{1,0:T(8,128)(2,1)S(1)}, bf16[128,512]{1,0:T(8,128)(2,1)S(1)}, u32[]{:S(2)}, u32[]{:S(2)}) collective-permute-start(bf16[128,512]{1,0:T(8,128)(2,1)S(1)} %get-tuple-element.20), channel_id=1, source_target_pairs={{0,1},{1,2},{2,3},{3,0},{4,5},{5,6},{6,7},{7,4},{8,9},{9,10},{10,1... | collective-permute-start | bytes 393224 | tf_op jit(solution)/shard_map/ppermute | solution.py:177
  190.8 8.2 %collective-permute-done.13.refs_1_ = bf16[128,512]{1,0:T(8,128)(2,1)S(1)} collective-permute-done((bf16[128,512]{1,0:T(8,128)(2,1)S(1)}, bf16[128,512]{1,0:T(8,128)(2,1)S(1)}, u32[]{:S(2)}, u32[]{:S(2)}) %collective-permute-start.13) | collective-permute-done | bytes 131104 | tf_op jit(solution)/shard_map/ppermute | solution.py:177
  206.4 12.2 %project_and_norm.3 = (bf16[128,4096]{1,0:T(8,128)(2,1)}, bf16[128,4096]{1,0:T(8,128)(2,1)}) custom-call(bf16[128,512]{1,0:T(8,128)(2,1)} %get-tuple-element.21.refs_0_, bf16[128,512]{1,0:T(8,128)(2,1)} %copy-done.8, bf16[128,512]{1,0:T(8,128)(2,1)} %copy-done.9, bf16[128,512]{1,0:T(8,128)(2,1)} %copy-done.10, bf16[8,512,512]{2,1,0:T(8,128)(2,1)} %bitcast.90, ...), custom_call_target="tpu_custom_call" | custom-call | flops 2147483648 | bytes 19922944 | tf_op jit(solution)/shard_map/project_and_norm/pallas_call | solution.py:114
  218.6 5.1 %collective-permute-start.16 = (bf16[128,4096]{1,0:T(8,128)(2,1)}, bf16[128,4096]{1,0:T(8,128)(2,1)}, u32[]{:S(2)}, u32[]{:S(2)}) collective-permute-start(bf16[128,4096]{1,0:T(8,128)(2,1)} %get-tuple-element.13), channel_id=1, source_target_pairs={{0,1},{1,2},{2,3},{4,5},{5,6},{6,7},{8,9},{9,10},{10,11},{12,13},{... | collective-permute-start | bytes 3145736 | tf_op jit(solution)/shard_map/ppermute | solution.py:185
  225.1 4.1 %collective-permute-start.20 = (bf16[128,4096]{1,0:T(8,128)(2,1)}, bf16[128,4096]{1,0:T(8,128)(2,1)}, u32[]{:S(2)}, u32[]{:S(2)}) collective-permute-start(bf16[128,4096]{1,0:T(8,128)(2,1)} %get-tuple-element.13), channel_id=1, source_target_pairs={{0,3},{3,0},{4,7},{7,4},{8,11},{11,8},{12,15},{15,12},{16,19},{19,... | collective-permute-start | bytes 3145736 | tf_op jit(solution)/shard_map/ppermute | solution.py:185
  230.0 21.2 %project_and_norm.2 = (bf16[512,4096]{1,0:T(8,128)(2,1)}, bf16[512,4096]{1,0:T(8,128)(2,1)}) custom-call(bf16[512,512]{1,0:T(8,128)(2,1)} %bitcast.2.refs_0_, bf16[512,512]{1,0:T(8,128)(2,1)} %collective-permute-done.2.refs_1_, bf16[512,512]{1,0:T(8,128)(2,1)} %collective-permute-done.3.refs_2_, bf16[512,512]{1,0:T(8,128)(2,1)} %copy-done.11, ...), custom_call_target="tpu_custom_call" | custom-call | flops 8589934592 | bytes 29360128 | tf_op jit(solution)/shard_map/project_and_norm/pallas_call | solution.py:114
  254.8 16.6 %collective-permute-done.17 = bf16[128,4096]{1,0:T(8,128)(2,1)} collective-permute-done((bf16[128,4096]{1,0:T(8,128)(2,1)}, bf16[128,4096]{1,0:T(8,128)(2,1)}, u32[]{:S(2)}, u32[]{:S(2)}) %collective-permute-start.17) | collective-permute-done | bytes 1048608 | tf_op jit(solution)/shard_map/ppermute | solution.py:185
  271.4 10.9 %convolution_convert_fusion.1 = bf16[512,1536]{1,0:T(8,128)(2,1)S(1)} fusion(bf16[512,4096]{1,0:T(8,128)(2,1)} %get-tuple-element.14, bf16[4096,1536]{0,1:T(8,128)(2,1)} %all-gather.6.cloned.1.call-done), kind=kOutput, calls=%fused_computation.1 | convolution fusion | flops 6443237376 | bytes 18350080 | tf_op jit(solution)/shard_map/dot_general | solution.py:286
  293.9 20.8 %collective-permute-done.18 = bf16[128,4096]{1,0:T(8,128)(2,1)S(1)} collective-permute-done((bf16[128,4096]{1,0:T(8,128)(2,1)}, bf16[128,4096]{1,0:T(8,128)(2,1)S(1)}, u32[]{:S(2)}, u32[]{:S(2)}) %collective-permute-start.18) | collective-permute-done | bytes 1048608 | tf_op jit(solution)/shard_map/ppermute | solution.py:185
  318.4 11.0 %convolution_convert_fusion = bf16[512,1536]{1,0:T(8,128)(2,1)S(1)} fusion(bf16[512,4096]{1,0:T(8,128)(2,1)} %bitcast.38, bf16[4096,1536]{0,1:T(8,128)(2,1)} %all-gather.6.cloned.1.call-done), kind=kOutput, calls=%fused_computation | convolution fusion | flops 6443237376 | bytes 18350080 | tf_op jit(solution)/shard_map/dot_general | solution.py:286
  330.7 3.9 all-to-all-start.2
  334.6 5.0 %column_attention.2 = bf16[512,512]{1,0:T(8,128)(2,1)} custom-call(bf16[512,1536]{1,0:T(8,128)(2,1)} %bitcast.84), custom_call_target="tpu_custom_call" | custom-call | flops 268435456 | bytes 2097152 | tf_op jit(solution)/shard_map/column_attention/pallas_call | solution.py:152
  339.6 16.0 %all-to-all-done.2 = bf16[8,2,32,1536]{3,2,1,0:T(8,128)(2,1)S(1)} async-done(((bf16[8,2,32,1536]{3,2,1,0:T(8,128)(2,1)}), bf16[8,2,32,1536]{3,2,1,0:T(8,128)(2,1)S(1)}, u32[]{:S(2)}, u32[]{:S(2)}) %all-to-all-start.2) | async-done | bytes 1572896 | tf_op jit(solution)/shard_map/all_to_all | solution.py:288
  360.4 5.0 %column_attention.3 = bf16[512,512]{1,0:T(8,128)(2,1)} custom-call(bf16[512,1536]{1,0:T(8,128)(2,1)} %bitcast.85), custom_call_target="tpu_custom_call" | custom-call | flops 268435456 | bytes 2097152 | tf_op jit(solution)/shard_map/column_attention/pallas_call | solution.py:152
  375.0 6.9 %all-to-all-done.3 = bf16[8,2,32,512]{3,2,1,0:T(8,128)(2,1)S(1)} async-done(((bf16[8,2,32,512]{3,2,1,0:T(8,128)(2,1)}), bf16[8,2,32,512]{3,2,1,0:T(8,128)(2,1)S(1)}, u32[]{:S(2)}, u32[]{:S(2)}) %all-to-all-start.3) | async-done | bytes 524320 | tf_op jit(solution)/shard_map/all_to_all | solution.py:295
  (96 shorter events, 72.5 us)
Async XLA Ops:
  7.2 198.6 %all-gather.8.cloned.1.call-start = ((), (), s32[]{:S(2)}) async-start(), calls=%async_computation.5 | async-start | bytes 4718592 | tf_op jit(solution)/shard_map/all_gather | solution.py:226
  7.9 197.9 %all-gather.10.cloned.1.call-start = ((), (), s32[]{:S(2)}) async-start(), calls=%async_computation.6 | async-start | bytes 14155776 | tf_op jit(solution)/shard_map/all_gather | solution.py:258
  9.0 19.7 %collective-permute-start = (bf16[512,512]{1,0:T(8,128)(2,1)S(1)}, bf16[512,512]{1,0:T(8,128)(2,1)S(1)}, u32[]{:S(2)}, u32[]{:S(2)}) collective-permute-start(bf16[512,512]{1,0:T(8,128)(2,1)S(1)} %slice.18), channel_id=1, source_target_pairs={{0,4},{4,8},{8,12},{12,16},{16,20},{20,24},{24,28},{1,5},{5,9},{9,... | collective-permute-start | bytes 1572872 | tf_op jit(solution)/shard_map/ppermute | solution.py:172
  12.5 16.3 %collective-permute-start.1 = (bf16[512,512]{1,0:T(8,128)(2,1)S(1)}, bf16[512,512]{1,0:T(8,128)(2,1)S(1)}, u32[]{:S(2)}, u32[]{:S(2)}) collective-permute-start(bf16[512,512]{1,0:T(8,128)(2,1)S(1)} %slice.19), channel_id=1, source_target_pairs={{0,4},{4,8},{8,12},{12,16},{16,20},{20,24},{24,28},{1,5},{5,9},{9,... | collective-permute-start | bytes 1572872 | tf_op jit(solution)/shard_map/ppermute | solution.py:172
  17.0 20.8 %collective-permute-start.5 = (bf16[512,512]{1,0:T(8,128)(2,1)}, bf16[512,512]{1,0:T(8,128)(2,1)}, u32[]{:S(2)}, u32[]{:S(2)}) collective-permute-start(bf16[512,512]{1,0:T(8,128)(2,1)} %param.11), channel_id=1, source_target_pairs={{0,1},{1,2},{2,3},{3,0},{4,5},{5,6},{6,7},{7,4},{8,9},{9,10},{10,1... | collective-permute-start | bytes 1572872 | tf_op jit(solution)/shard_map/ppermute | solution.py:177
  18.7 37.0 %collective-permute-start.6 = (bf16[512,512]{1,0:T(8,128)(2,1)}, bf16[512,512]{1,0:T(8,128)(2,1)}, u32[]{:S(2)}, u32[]{:S(2)}) collective-permute-start(bf16[512,512]{1,0:T(8,128)(2,1)} %param.11), channel_id=1, source_target_pairs={{0,2},{1,3},{2,0},{3,1},{4,6},{5,7},{6,4},{7,5},{8,10},{9,11},{10,... | collective-permute-start | bytes 1572872 | tf_op jit(solution)/shard_map/ppermute | solution.py:177
  21.2 34.4 %collective-permute-start.7 = (bf16[512,512]{1,0:T(8,128)(2,1)}, bf16[512,512]{1,0:T(8,128)(2,1)}, u32[]{:S(2)}, u32[]{:S(2)}) collective-permute-start(bf16[512,512]{1,0:T(8,128)(2,1)} %param.11), channel_id=1, source_target_pairs={{0,3},{1,0},{2,1},{3,2},{4,7},{5,4},{6,5},{7,6},{8,11},{9,8},{10,9... | collective-permute-start | bytes 1572872 | tf_op jit(solution)/shard_map/ppermute | solution.py:177
  58.5 212.8 %all-gather.6.cloned.1.call-start = ((), (), s32[]{:S(2)}) async-start(), calls=%async_computation.4 | async-start | bytes 14155776 | tf_op jit(solution)/shard_map/all_gather | solution.py:259
  63.8 76.7 %collective-permute-start.8 = (bf16[128,4096]{1,0:T(8,128)(2,1)}, bf16[128,4096]{1,0:T(8,128)(2,1)}, u32[]{:S(2)}, u32[]{:S(2)}) collective-permute-start(bf16[128,4096]{1,0:T(8,128)(2,1)} %get-tuple-element.16), channel_id=1, source_target_pairs={{0,1},{1,2},{2,3},{4,5},{5,6},{6,7},{8,9},{9,10},{10,11},{12,13},{... | collective-permute-start | bytes 3145736 | tf_op jit(solution)/shard_map/ppermute | solution.py:185
  78.4 60.8 %collective-permute-start.9 = (bf16[128,4096]{1,0:T(8,128)(2,1)}, bf16[128,4096]{1,0:T(8,128)(2,1)}, u32[]{:S(2)}, u32[]{:S(2)}) collective-permute-start(bf16[128,4096]{1,0:T(8,128)(2,1)} %get-tuple-element.16), channel_id=1, source_target_pairs={{1,0},{2,1},{3,2},{5,4},{6,5},{7,6},{9,8},{10,9},{11,10},{13,12},{... | collective-permute-start | bytes 3145736 | tf_op jit(solution)/shard_map/ppermute | solution.py:185
  79.7 119.4 %collective-permute-start.12 = (bf16[128,4096]{1,0:T(8,128)(2,1)}, bf16[128,4096]{1,0:T(8,128)(2,1)}, u32[]{:S(2)}, u32[]{:S(2)}) collective-permute-start(bf16[128,4096]{1,0:T(8,128)(2,1)} %get-tuple-element.16), channel_id=1, source_target_pairs={{0,3},{3,0},{4,7},{7,4},{8,11},{11,8},{12,15},{15,12},{16,19},{19,... | collective-permute-start | bytes 3145736 | tf_op jit(solution)/shard_map/ppermute | solution.py:185
  86.8 138.3 %collective-permute-start.2 = (bf16[512,512]{1,0:T(8,128)(2,1)}, bf16[512,512]{1,0:T(8,128)(2,1)}, u32[]{:S(2)}, u32[]{:S(2)}) collective-permute-start(bf16[512,512]{1,0:T(8,128)(2,1)} %bitcast.2.refs_0_), channel_id=1, source_target_pairs={{0,1},{1,2},{2,3},{3,0},{4,5},{5,6},{6,7},{7,4},{8,9},{9,10},{10,1... | collective-permute-start | bytes 1572872 | tf_op jit(solution)/shard_map/ppermute | solution.py:177
  86.8 142.4 %collective-permute-start.3 = (bf16[512,512]{1,0:T(8,128)(2,1)}, bf16[512,512]{1,0:T(8,128)(2,1)}, u32[]{:S(2)}, u32[]{:S(2)}) collective-permute-start(bf16[512,512]{1,0:T(8,128)(2,1)} %bitcast.2.refs_0_), channel_id=1, source_target_pairs={{0,2},{1,3},{2,0},{3,1},{4,6},{5,7},{6,4},{7,5},{8,10},{9,11},{10,... | collective-permute-start | bytes 1572872 | tf_op jit(solution)/shard_map/ppermute | solution.py:177
  139.2 35.2 %collective-permute-start.10 = (bf16[128,4096]{1,0:T(8,128)(2,1)}, bf16[128,4096]{1,0:T(8,128)(2,1)S(1)}, u32[]{:S(2)}, u32[]{:S(2)}) collective-permute-start(bf16[128,4096]{1,0:T(8,128)(2,1)} %collective-permute-done.9), channel_id=1, source_target_pairs={{2,1},{1,0},{6,5},{5,4},{10,9},{9,8},{14,13},{13,12},{18,17},{17,1... | collective-permute-start | bytes 3145736 | tf_op jit(solution)/shard_map/ppermute | solution.py:185
  140.5 33.9 %collective-permute-start.11 = (bf16[128,4096]{1,0:T(8,128)(2,1)}, bf16[128,4096]{1,0:T(8,128)(2,1)S(1)}, u32[]{:S(2)}, u32[]{:S(2)}) collective-permute-start(bf16[128,4096]{1,0:T(8,128)(2,1)} %collective-permute-done.8), channel_id=1, source_target_pairs={{1,2},{2,3},{5,6},{6,7},{9,10},{10,11},{13,14},{14,15},{17,18},{18... | collective-permute-start | bytes 3145736 | tf_op jit(solution)/shard_map/ppermute | solution.py:185
  174.4 54.8 %collective-permute-start.4 = (bf16[512,512]{1,0:T(8,128)(2,1)}, bf16[512,512]{1,0:T(8,128)(2,1)S(1)}, u32[]{:S(2)}, u32[]{:S(2)}) collective-permute-start(bf16[512,512]{1,0:T(8,128)(2,1)} %bitcast.2.refs_0_), channel_id=1, source_target_pairs={{0,3},{1,0},{2,1},{3,2},{4,7},{5,4},{6,5},{7,6},{8,11},{9,8},{10,9... | collective-permute-start | bytes 1572872 | tf_op jit(solution)/shard_map/ppermute | solution.py:177
  174.4 24.6 %collective-permute-start.13 = (bf16[128,512]{1,0:T(8,128)(2,1)S(1)}, bf16[128,512]{1,0:T(8,128)(2,1)S(1)}, u32[]{:S(2)}, u32[]{:S(2)}) collective-permute-start(bf16[128,512]{1,0:T(8,128)(2,1)S(1)} %get-tuple-element.20), channel_id=1, source_target_pairs={{0,1},{1,2},{2,3},{3,0},{4,5},{5,6},{6,7},{7,4},{8,9},{9,10},{10,1... | collective-permute-start | bytes 393224 | tf_op jit(solution)/shard_map/ppermute | solution.py:177
  218.6 36.2 %collective-permute-start.16 = (bf16[128,4096]{1,0:T(8,128)(2,1)}, bf16[128,4096]{1,0:T(8,128)(2,1)}, u32[]{:S(2)}, u32[]{:S(2)}) collective-permute-start(bf16[128,4096]{1,0:T(8,128)(2,1)} %get-tuple-element.13), channel_id=1, source_target_pairs={{0,1},{1,2},{2,3},{4,5},{5,6},{6,7},{8,9},{9,10},{10,11},{12,13},{... | collective-permute-start | bytes 3145736 | tf_op jit(solution)/shard_map/ppermute | solution.py:185
  223.8 47.6 %collective-permute-start.17 = (bf16[128,4096]{1,0:T(8,128)(2,1)}, bf16[128,4096]{1,0:T(8,128)(2,1)}, u32[]{:S(2)}, u32[]{:S(2)}) collective-permute-start(bf16[128,4096]{1,0:T(8,128)(2,1)} %get-tuple-element.13), channel_id=1, source_target_pairs={{1,0},{2,1},{3,2},{5,4},{6,5},{7,6},{9,8},{10,9},{11,10},{13,12},{... | collective-permute-start | bytes 3145736 | tf_op jit(solution)/shard_map/ppermute | solution.py:185
  225.1 90.9 %collective-permute-start.20 = (bf16[128,4096]{1,0:T(8,128)(2,1)}, bf16[128,4096]{1,0:T(8,128)(2,1)}, u32[]{:S(2)}, u32[]{:S(2)}) collective-permute-start(bf16[128,4096]{1,0:T(8,128)(2,1)} %get-tuple-element.13), channel_id=1, source_target_pairs={{0,3},{3,0},{4,7},{7,4},{8,11},{11,8},{12,15},{15,12},{16,19},{19,... | collective-permute-start | bytes 3145736 | tf_op jit(solution)/shard_map/ppermute | solution.py:185
  283.6 47.1 %all-to-all-start = ((bf16[8,2,32,1536]{3,2,1,0:T(8,128)(2,1)}), bf16[8,2,32,1536]{3,2,1,0:T(8,128)(2,1)S(1)}, u32[]{:S(2)}, u32[]{:S(2)}) async-start(bf16[8,2,32,1536]{3,2,1,0:T(8,128)(2,1)} %bitcast.77), calls=%async_computation | async-start | bytes 3145728 | tf_op jit(solution)/shard_map/all_to_all | solution.py:288
  287.2 27.6 %collective-permute-start.18 = (bf16[128,4096]{1,0:T(8,128)(2,1)}, bf16[128,4096]{1,0:T(8,128)(2,1)S(1)}, u32[]{:S(2)}, u32[]{:S(2)}) collective-permute-start(bf16[128,4096]{1,0:T(8,128)(2,1)} %collective-permute-done.17), channel_id=1, source_target_pairs={{2,1},{1,0},{6,5},{5,4},{10,9},{9,8},{14,13},{13,12},{18,17},{17,1... | collective-permute-start | bytes 3145736 | tf_op jit(solution)/shard_map/ppermute | solution.py:185
  288.6 26.1 %collective-permute-start.19 = (bf16[128,4096]{1,0:T(8,128)(2,1)}, bf16[128,4096]{1,0:T(8,128)(2,1)S(1)}, u32[]{:S(2)}, u32[]{:S(2)}) collective-permute-start(bf16[128,4096]{1,0:T(8,128)(2,1)} %collective-permute-done.16), channel_id=1, source_target_pairs={{1,2},{2,3},{5,6},{6,7},{9,10},{10,11},{13,14},{14,15},{17,18},{18... | collective-permute-start | bytes 3145736 | tf_op jit(solution)/shard_map/ppermute | solution.py:185
  330.7 24.9 %all-to-all-start.2 = ((bf16[8,2,32,1536]{3,2,1,0:T(8,128)(2,1)}), bf16[8,2,32,1536]{3,2,1,0:T(8,128)(2,1)S(1)}, u32[]{:S(2)}, u32[]{:S(2)}) async-start(bf16[8,2,32,1536]{3,2,1,0:T(8,128)(2,1)} %bitcast.86), calls=%async_computation.2 | async-start | bytes 3145728 | tf_op jit(solution)/shard_map/all_to_all | solution.py:288
  (16 other events, 78.1 us)
Sparse Core Ops, SparseCore 0:
  9.9 42.0 all-gather.7
  58.6 81.5 all-gather.9
  142.1 74.5 all-gather.5

commit v3 on v2

--- a/solution.py
+++ b/solution.py
@@ -186,18 +186,15 @@
 
 
 def line_first(array):
-    return (
-        moved(array, [(0, 1), (1, 2), (2, 3)]),
-        moved(array, [(1, 0), (2, 1), (3, 2)]),
-        moved(array, [(0, 3), (3, 0)]),
-    )
-
-
-def line_second(array, below, above, across):
+    return moved(array, [(0, 1), (1, 2), (2, 3)]), moved(array, [(1, 0), (2, 1), (3, 2)])
+
+
+def line_second(array, below, above):
     place = lax.axis_index("head")
     at_end = (place == 0) | (place == 3)
     below_two = moved(below, [(1, 2), (2, 3)])
     above_two = moved(above, [(2, 1), (1, 0)])
+    across = moved(array, [(0, 3), (3, 0)])
     slots = [
         (below, (place + 3) % 4),
         (above, (place + 1) % 4),
@@ -229,7 +226,8 @@
     key_back, value_back = passed_along((row_keys[-COLS:], row_values[-COLS:]), "seq", 1)
     halves = residual_in.reshape(share // block, 2, block // 2, model)
     residual_own = halves[:, 0].reshape(half, model)
-    residual_first = line_second(residual_own, *line_first(residual_own))
+    residual_copies = line_first(residual_own)
+    residual_first = line_second(residual_own, *residual_copies)
 
     first_row = (lax.axis_index("seq") * lines).reshape(1)
     row_out = [
@@ -253,7 +251,7 @@
             )
         )
     row_out = jnp.concatenate(row_out, 0)
-    far_weight = after(far_weight, row_out)
+    far_weight = after(far_weight, row_out, *residual_copies)
     qkv_own = after(qkv_weight.reshape(qkv_weight.shape[0], -1), far_weight)
     far_weight = lax.all_gather(far_weight, "seq")
     qkv_flat = lax.all_gather(qkv_own, "seq", axis=0, tiled=True)
@@ -278,7 +276,6 @@
     )
     out_first = lax.dynamic_slice_in_dim(out_first, place * half, half, 0)
     copies = line_first(normed_last)
-    normed_first = after(normed_first, *copies[:2])
     normed_last = line_second(normed_last, *copies).reshape(heads * half, model)
 
     def attend(normed):

time: 391 us -> 374 us (0.957)
  local copies, waits for them, and re-layouts: 30.5 us -> 23.7 us
  starting transfers between devices: 80.1 us -> 73.9 us
  matrix products: 21.9 us -> 17.7 us
    ppermute x9, waiting for transfers between devices: 29.1 us -> 63.8 us  [from_behind(): lax.ppermute(array, 'head', [(i, (i + by) % size) for i in range(size)])]
    ppermute x10, waiting for transfers between devices: 119 us -> 85.8 us  [moved(): return lax.ppermute(value, 'head', pairs)]
    ppermute x10, starting transfers between devices: 36.2 us -> 22.7 us  [moved(): return lax.ppermute(value, 'head', pairs)]
    ppermute x9, starting transfers between devices: 22.4 us -> 29.7 us  [from_behind(): lax.ppermute(array, 'head', [(i, (i + by) % size) for i in range(size)])]
    dynamic_update_slice x4, local copies, waits for them, and re-layouts: 7.26 us -> 2.91 us  [line_second(): gathered = lax.dynamic_update_index_in_dim(gathered, value, slot, 0)]
    dot_general x2, matrix products: 21.9 us -> 17.7 us  [attend(): projected = jnp.dot(normed, qkv_flat, preferred_element_type=jnp.float32)]
    unnamed x25 -> x33, local copies, waits for them, and re-layouts: 8.85 us -> 7.78 us
  transfers between devices with their start and end apart: 28 -> 28, of which waited for: 10 -> 10; matrix products, arithmetic and copies ran while one was open for 15% -> 13% of each run, Pallas kernels for 14% -> 15%
where the time goes in v3:
time: 374 us; the launch traced here: 373 us
  waiting for transfers between devices  176 us (47%)
  starting transfers between devices  73.9 us (20%)
  Pallas kernels  56.4 us (15%)
  local copies, waits for them, and re-layouts  23.7 us (6%)
  matrix products  17.7 us (5%)
  between operations  14.3 us (4%)
  other arithmetic  10.4 us (3%)
    ppermute x10, waiting for transfers between devices, moved(): return lax.ppermute(value, 'head', pairs)  85.8 us
    ppermute x9, waiting for transfers between devices, from_behind(): lax.ppermute(array, 'head', [(i, (i + by) % size) for i in range(size)])  63.8 us
    pallas_call x2, Pallas kernels, project_and_norm(): pl.pallas_call(functools.partial(project_kernel, parts, width), grid=(ste...  33.8 us
    ppermute x9, starting transfers between devices, from_behind(): lax.ppermute(array, 'head', [(i, (i + by) % size) for i in range(size)])  29.7 us
    ppermute x10, starting transfers between devices, moved(): return lax.ppermute(value, 'head', pairs)  22.7 us
    dot_general x2, matrix products, attend(): projected = jnp.dot(normed, qkv_flat, preferred_element_type=jnp.float32)  17.7 us
    all_to_all x2, waiting for transfers between devices, attend(): lax.all_to_all(qkv.transpose(1, 0, 2, 3), 'seq', split_axis=0, concat_axi...  15.9 us
    pallas_call x2, Pallas kernels, band_attention(): pl.pallas_call(band_kernel, grid_spec=pltpu.PrefetchScalarGridSpec(num_sc...  12.4 us
  transfers between devices with their start and end apart: 28, of which 10 were waited for; matrix products, arithmetic and copies ran while one was open for 13% of the time, Pallas kernels for 15%

profile of v3, /device:TPU:0, one launch (start us, length us, event | category | flops | bytes accessed | tf_op | source)
XLA Modules:
  0.0 372.7 jit_solution(16006232468401574776)
XLA Ops:
  12.5 4.5 %collective-permute-start.1 = (bf16[512,512]{1,0:T(8,128)(2,1)S(1)}, bf16[512,512]{1,0:T(8,128)(2,1)S(1)}, u32[]{:S(2)}, u32[]{:S(2)}) collective-permute-start(bf16[512,512]{1,0:T(8,128)(2,1)S(1)} %slice.19), channel_id=1, source_target_pairs={{0,4},{4,8},{8,12},{12,16},{16,20},{20,24},{24,28},{1,5},{5,9},{9,... | collective-permute-start | bytes 1572872 | tf_op jit(solution)/shard_map/ppermute | solution.py:172
  24.9 4.7 %collective-permute-start.7 = (bf16[512,512]{1,0:T(8,128)(2,1)}, bf16[512,512]{1,0:T(8,128)(2,1)}, u32[]{:S(2)}, u32[]{:S(2)}) collective-permute-start(bf16[512,512]{1,0:T(8,128)(2,1)} %param.11), channel_id=1, source_target_pairs={{0,3},{1,0},{2,1},{3,2},{4,7},{5,4},{6,5},{7,6},{8,11},{9,8},{10,9... | collective-permute-start | bytes 1572872 | tf_op jit(solution)/shard_map/ppermute | solution.py:177
  30.6 6.2 %band_attention.3 = bf16[512,512]{1,0:T(8,128)(2,1)} custom-call(s32[1]{0:T(128)S(6)} %add.63.first_ref, bf16[1024,512]{1,0:T(8,128)(2,1)} %q_ref.3, bf16[1024,512]{1,0:T(8,128)(2,1)} %kc_ref.3, bf16[1024,512]{1,0:T(8,128)(2,1)} %kc_ref.3, bf16[1024,512]{1,0:T(8,128)(2,1)} %vc_ref.3, bf16[1024,512]{1,0:T(8,128)(2,1)} %vc_ref.3), custom_call_target="tpu_custom_call" | custom-call | flops 805306368 | bytes 3145728 | tf_op jit(solution)/shard_map/band_attention/pallas_call | solution.py:60
  36.8 6.3 %band_attention.2 = bf16[512,512]{1,0:T(8,128)(2,1)} custom-call(s32[1]{0:T(128)} %bitcast.first_ref, bf16[1024,512]{1,0:T(8,128)(2,1)} %q_ref.3, bf16[512,512]{1,0:T(8,128)(2,1)} %copy-done.10, bf16[1024,512]{1,0:T(8,128)(2,1)} %kc_ref.3, bf16[512,512]{1,0:T(8,128)(2,1)} %copy-done.11, bf16[1024,512]{1,0:T(8,128)(2,1)} %vc_ref.3), custom_call_target="tpu_custom_call" | custom-call | flops 805306368 | bytes 3145728 | tf_op jit(solution)/shard_map/band_attention/pallas_call | solution.py:60
  44.2 18.0 %collective-permute-done.7 = bf16[512,512]{1,0:T(8,128)(2,1)} collective-permute-done((bf16[512,512]{1,0:T(8,128)(2,1)}, bf16[512,512]{1,0:T(8,128)(2,1)}, u32[]{:S(2)}, u32[]{:S(2)}) %collective-permute-start.7) | collective-permute-done | bytes 524320 | tf_op jit(solution)/shard_map/ppermute | solution.py:177
  62.2 34.3 %collective-permute-done.6 = bf16[512,512]{1,0:T(8,128)(2,1)} collective-permute-done((bf16[512,512]{1,0:T(8,128)(2,1)}, bf16[512,512]{1,0:T(8,128)(2,1)}, u32[]{:S(2)}, u32[]{:S(2)}) %collective-permute-start.6) | collective-permute-done | bytes 524320 | tf_op jit(solution)/shard_map/ppermute | solution.py:177
  100.6 3.9 %copy.31 = bf16[512,4,3,128]{0,3,2,1:T(8,128)(2,1)} copy(bf16[512,4,3,128]{3,1,2,0:T(4,128)(2,1)} %param.13) | data formatting | bytes 3145728 | tf_op args[6]
  108.0 4.4 %collective-permute-start.3 = (bf16[512,512]{1,0:T(8,128)(2,1)}, bf16[512,512]{1,0:T(8,128)(2,1)}, u32[]{:S(2)}, u32[]{:S(2)}) collective-permute-start(bf16[512,512]{1,0:T(8,128)(2,1)} %bitcast.2.refs_0_), channel_id=1, source_target_pairs={{0,2},{1,3},{2,0},{3,1},{4,6},{5,7},{6,4},{7,5},{8,10},{9,11},{10,... | collective-permute-start | bytes 1572872 | tf_op jit(solution)/shard_map/ppermute | solution.py:177
  115.4 61.9 %collective-permute-done.10 = bf16[128,4096]{1,0:T(8,128)(2,1)S(1)} collective-permute-done((bf16[128,4096]{1,0:T(8,128)(2,1)S(1)}, bf16[128,4096]{1,0:T(8,128)(2,1)S(1)}, u32[]{:S(2)}, u32[]{:S(2)}) %collective-permute-start.10) | collective-permute-done | bytes 1048608 | tf_op jit(solution)/shard_map/ppermute | solution.py:185
  177.2 19.6 %collective-permute-start.13 = (bf16[128,512]{1,0:T(8,128)(2,1)S(1)}, bf16[128,512]{1,0:T(8,128)(2,1)S(1)}, u32[]{:S(2)}, u32[]{:S(2)}) collective-permute-start(bf16[128,512]{1,0:T(8,128)(2,1)S(1)} %get-tuple-element.18), channel_id=1, source_target_pairs={{0,1},{1,2},{2,3},{3,0},{4,5},{5,6},{6,7},{7,4},{8,9},{9,10},{10,1... | collective-permute-start | bytes 393224 | tf_op jit(solution)/shard_map/ppermute | solution.py:177
  197.1 7.8 %collective-permute-done.13.refs_1_ = bf16[128,512]{1,0:T(8,128)(2,1)S(1)} collective-permute-done((bf16[128,512]{1,0:T(8,128)(2,1)S(1)}, bf16[128,512]{1,0:T(8,128)(2,1)S(1)}, u32[]{:S(2)}, u32[]{:S(2)}) %collective-permute-start.13) | collective-permute-done | bytes 131104 | tf_op jit(solution)/shard_map/ppermute | solution.py:177
  208.6 3.7 collective-permute-done.14.refs_2_
  212.9 12.0 %project_and_norm.3 = (bf16[128,4096]{1,0:T(8,128)(2,1)}, bf16[128,4096]{1,0:T(8,128)(2,1)}) custom-call(bf16[128,512]{1,0:T(8,128)(2,1)} %get-tuple-element.19.refs_0_, bf16[128,512]{1,0:T(8,128)(2,1)} %copy-done.12, bf16[128,512]{1,0:T(8,128)(2,1)} %copy-done.13, bf16[128,512]{1,0:T(8,128)(2,1)} %copy-done.14, bf16[8,512,512]{2,1,0:T(8,128)(2,1)} %bitcast.91, ...), custom_call_target="tpu_custom_call" | custom-call | flops 2147483648 | bytes 19922944 | tf_op jit(solution)/shard_map/project_and_norm/pallas_call | solution.py:114
  224.9 5.1 %collective-permute-start.16 = (bf16[128,4096]{1,0:T(8,128)(2,1)}, bf16[128,4096]{1,0:T(8,128)(2,1)}, u32[]{:S(2)}, u32[]{:S(2)}) collective-permute-start(bf16[128,4096]{1,0:T(8,128)(2,1)} %get-tuple-element.13), channel_id=1, source_target_pairs={{0,1},{1,2},{2,3},{4,5},{5,6},{6,7},{8,9},{9,10},{10,11},{12,13},{... | collective-permute-start | bytes 3145736 | tf_op jit(solution)/shard_map/ppermute | solution.py:185
  231.3 5.5 %collective-permute-start.20 = (bf16[128,4096]{1,0:T(8,128)(2,1)}, bf16[128,4096]{1,0:T(8,128)(2,1)}, u32[]{:S(2)}, u32[]{:S(2)}) collective-permute-start(bf16[128,4096]{1,0:T(8,128)(2,1)} %get-tuple-element.13), channel_id=1, source_target_pairs={{0,3},{3,0},{4,7},{7,4},{8,11},{11,8},{12,15},{15,12},{16,19},{19,... | collective-permute-start | bytes 3145736 | tf_op jit(solution)/shard_map/ppermute | solution.py:185
  236.8 21.8 %project_and_norm.2 = (bf16[512,4096]{1,0:T(8,128)(2,1)}, bf16[512,4096]{1,0:T(8,128)(2,1)}) custom-call(bf16[512,512]{1,0:T(8,128)(2,1)} %bitcast.2.refs_0_, bf16[512,512]{1,0:T(8,128)(2,1)} %collective-permute-done.2.refs_1_, bf16[512,512]{1,0:T(8,128)(2,1)} %collective-permute-done.3.refs_2_, bf16[512,512]{1,0:T(8,128)(2,1)} %collective-permute-done.4.refs_3_, ...), custom_call_target="tpu_custom_call" | custom-call | flops 8589934592 | bytes 29360128 | tf_op jit(solution)/shard_map/project_and_norm/pallas_call | solution.py:114
  258.6 10.9 %convolution_convert_fusion.1 = bf16[512,1536]{1,0:T(8,128)(2,1)S(1)} fusion(bf16[512,4096]{1,0:T(8,128)(2,1)} %get-tuple-element.11, bf16[4096,1536]{0,1:T(8,128)(2,1)} %all-gather.6.cloned.1.call-done), kind=kOutput, calls=%fused_computation.1 | convolution fusion | flops 6443237376 | bytes 18350080 | tf_op jit(solution)/shard_map/dot_general | solution.py:283
  270.8 3.9 %all-to-all-start = ((bf16[8,2,32,1536]{3,2,1,0:T(8,128)(2,1)}), bf16[8,2,32,1536]{3,2,1,0:T(8,128)(2,1)S(1)}, u32[]{:S(2)}, u32[]{:S(2)}) async-start(bf16[8,2,32,1536]{3,2,1,0:T(8,128)(2,1)} %bitcast.77), calls=%async_computation | async-start | bytes 3145728 | tf_op jit(solution)/shard_map/all_to_all | solution.py:285
  283.6 20.6 %collective-permute-done.18 = bf16[128,4096]{1,0:T(8,128)(2,1)S(1)} collective-permute-done((bf16[128,4096]{1,0:T(8,128)(2,1)}, bf16[128,4096]{1,0:T(8,128)(2,1)S(1)}, u32[]{:S(2)}, u32[]{:S(2)}) %collective-permute-start.18) | collective-permute-done | bytes 1048608 | tf_op jit(solution)/shard_map/ppermute | solution.py:185
  306.0 6.7 %convolution_convert_fusion = bf16[512,1536]{1,0:T(8,128)(2,1)S(1)} fusion(bf16[512,4096]{1,0:T(8,128)(2,1)S(1)} %bitcast.87, bf16[4096,1536]{0,1:T(8,128)(2,1)S(1)} %copy-done.15), kind=kOutput, calls=%fused_computation | convolution fusion | flops 6443237376 | bytes 18350080 | tf_op jit(solution)/shard_map/dot_general | solution.py:283
  317.6 5.0 %column_attention.2 = bf16[512,512]{1,0:T(8,128)(2,1)} custom-call(bf16[512,1536]{1,0:T(8,128)(2,1)} %bitcast.84), custom_call_target="tpu_custom_call" | custom-call | flops 268435456 | bytes 2097152 | tf_op jit(solution)/shard_map/column_attention/pallas_call | solution.py:152
  322.6 15.9 %all-to-all-done.2 = bf16[8,2,32,1536]{3,2,1,0:T(8,128)(2,1)S(1)} async-done(((bf16[8,2,32,1536]{3,2,1,0:T(8,128)(2,1)}), bf16[8,2,32,1536]{3,2,1,0:T(8,128)(2,1)S(1)}, u32[]{:S(2)}, u32[]{:S(2)}) %all-to-all-start.2) | async-done | bytes 1572896 | tf_op jit(solution)/shard_map/all_to_all | solution.py:285
  343.4 5.0 %column_attention.3 = bf16[512,512]{1,0:T(8,128)(2,1)} custom-call(bf16[512,1536]{1,0:T(8,128)(2,1)} %bitcast.85), custom_call_target="tpu_custom_call" | custom-call | flops 268435456 | bytes 2097152 | tf_op jit(solution)/shard_map/column_attention/pallas_call | solution.py:152
  358.0 6.9 %all-to-all-done.3 = bf16[8,2,32,512]{3,2,1,0:T(8,128)(2,1)S(1)} async-done(((bf16[8,2,32,512]{3,2,1,0:T(8,128)(2,1)}), bf16[8,2,32,512]{3,2,1,0:T(8,128)(2,1)S(1)}, u32[]{:S(2)}, u32[]{:S(2)}) %all-to-all-start.3) | async-done | bytes 524320 | tf_op jit(solution)/shard_map/all_to_all | solution.py:292
  (104 shorter events, 63.8 us)
Async XLA Ops:
  7.2 205.1 %all-gather.8.cloned.1.call-start = ((), (), s32[]{:S(2)}) async-start(), calls=%async_computation.5 | async-start | bytes 4718592 | tf_op jit(solution)/shard_map/all_gather | solution.py:223
  7.9 204.4 %all-gather.10.cloned.1.call-start = ((), (), s32[]{:S(2)}) async-start(), calls=%async_computation.6 | async-start | bytes 14155776 | tf_op jit(solution)/shard_map/all_gather | solution.py:256
  9.0 20.6 %collective-permute-start = (bf16[512,512]{1,0:T(8,128)(2,1)S(1)}, bf16[512,512]{1,0:T(8,128)(2,1)S(1)}, u32[]{:S(2)}, u32[]{:S(2)}) collective-permute-start(bf16[512,512]{1,0:T(8,128)(2,1)S(1)} %slice.18), channel_id=1, source_target_pairs={{0,4},{4,8},{8,12},{12,16},{16,20},{20,24},{24,28},{1,5},{5,9},{9,... | collective-permute-start | bytes 1572872 | tf_op jit(solution)/shard_map/ppermute | solution.py:172
  12.5 17.2 %collective-permute-start.1 = (bf16[512,512]{1,0:T(8,128)(2,1)S(1)}, bf16[512,512]{1,0:T(8,128)(2,1)S(1)}, u32[]{:S(2)}, u32[]{:S(2)}) collective-permute-start(bf16[512,512]{1,0:T(8,128)(2,1)S(1)} %slice.19), channel_id=1, source_target_pairs={{0,4},{4,8},{8,12},{12,16},{16,20},{20,24},{24,28},{1,5},{5,9},{9,... | collective-permute-start | bytes 1572872 | tf_op jit(solution)/shard_map/ppermute | solution.py:172
  20.1 79.1 %collective-permute-start.8 = (bf16[128,4096]{1,0:T(8,128)(2,1)}, bf16[128,4096]{1,0:T(8,128)(2,1)S(1)}, u32[]{:S(2)}, u32[]{:S(2)}) collective-permute-start(bf16[128,4096]{1,0:T(8,128)(2,1)} %get-tuple-element.15), channel_id=1, source_target_pairs={{0,1},{1,2},{2,3},{4,5},{5,6},{6,7},{8,9},{9,10},{10,11},{12,13},{... | collective-permute-start | bytes 3145736 | tf_op jit(solution)/shard_map/ppermute | solution.py:185
  23.6 75.6 %collective-permute-start.9 = (bf16[128,4096]{1,0:T(8,128)(2,1)}, bf16[128,4096]{1,0:T(8,128)(2,1)S(1)}, u32[]{:S(2)}, u32[]{:S(2)}) collective-permute-start(bf16[128,4096]{1,0:T(8,128)(2,1)} %get-tuple-element.15), channel_id=1, source_target_pairs={{1,0},{2,1},{3,2},{5,4},{6,5},{7,6},{9,8},{10,9},{11,10},{13,12},{... | collective-permute-start | bytes 3145736 | tf_op jit(solution)/shard_map/ppermute | solution.py:185
  24.9 37.3 %collective-permute-start.7 = (bf16[512,512]{1,0:T(8,128)(2,1)}, bf16[512,512]{1,0:T(8,128)(2,1)}, u32[]{:S(2)}, u32[]{:S(2)}) collective-permute-start(bf16[512,512]{1,0:T(8,128)(2,1)} %param.11), channel_id=1, source_target_pairs={{0,3},{1,0},{2,1},{3,2},{4,7},{5,4},{6,5},{7,6},{8,11},{9,8},{10,9... | collective-permute-start | bytes 1572872 | tf_op jit(solution)/shard_map/ppermute | solution.py:177
  29.7 66.8 %collective-permute-start.6 = (bf16[512,512]{1,0:T(8,128)(2,1)}, bf16[512,512]{1,0:T(8,128)(2,1)}, u32[]{:S(2)}, u32[]{:S(2)}) collective-permute-start(bf16[512,512]{1,0:T(8,128)(2,1)} %param.11), channel_id=1, source_target_pairs={{0,2},{1,3},{2,0},{3,1},{4,6},{5,7},{6,4},{7,5},{8,10},{9,11},{10,... | collective-permute-start | bytes 1572872 | tf_op jit(solution)/shard_map/ppermute | solution.py:177
  29.7 66.8 %collective-permute-start.5 = (bf16[512,512]{1,0:T(8,128)(2,1)}, bf16[512,512]{1,0:T(8,128)(2,1)}, u32[]{:S(2)}, u32[]{:S(2)}) collective-permute-start(bf16[512,512]{1,0:T(8,128)(2,1)} %param.11), channel_id=1, source_target_pairs={{0,1},{1,2},{2,3},{3,0},{4,5},{5,6},{6,7},{7,4},{8,9},{9,10},{10,1... | collective-permute-start | bytes 1572872 | tf_op jit(solution)/shard_map/ppermute | solution.py:177
  100.5 158.1 %all-gather.6.cloned.1.call-start = ((), (), s32[]{:S(2)}) async-start(), calls=%async_computation.4 | async-start | bytes 14155776 | tf_op jit(solution)/shard_map/all_gather | solution.py:257
  104.5 100.4 %collective-permute-start.12 = (bf16[128,4096]{1,0:T(8,128)(2,1)}, bf16[128,4096]{1,0:T(8,128)(2,1)}, u32[]{:S(2)}, u32[]{:S(2)}) collective-permute-start(bf16[128,4096]{1,0:T(8,128)(2,1)} %get-tuple-element.15), channel_id=1, source_target_pairs={{0,3},{3,0},{4,7},{7,4},{8,11},{11,8},{12,15},{15,12},{16,19},{19,... | collective-permute-start | bytes 3145736 | tf_op jit(solution)/shard_map/ppermute | solution.py:185
  108.0 123.3 %collective-permute-start.2 = (bf16[512,512]{1,0:T(8,128)(2,1)}, bf16[512,512]{1,0:T(8,128)(2,1)}, u32[]{:S(2)}, u32[]{:S(2)}) collective-permute-start(bf16[512,512]{1,0:T(8,128)(2,1)} %bitcast.2.refs_0_), channel_id=1, source_target_pairs={{0,1},{1,2},{2,3},{3,0},{4,5},{5,6},{6,7},{7,4},{8,9},{9,10},{10,1... | collective-permute-start | bytes 1572872 | tf_op jit(solution)/shard_map/ppermute | solution.py:177
  108.0 128.8 %collective-permute-start.3 = (bf16[512,512]{1,0:T(8,128)(2,1)}, bf16[512,512]{1,0:T(8,128)(2,1)}, u32[]{:S(2)}, u32[]{:S(2)}) collective-permute-start(bf16[512,512]{1,0:T(8,128)(2,1)} %bitcast.2.refs_0_), channel_id=1, source_target_pairs={{0,2},{1,3},{2,0},{3,1},{4,6},{5,7},{6,4},{7,5},{8,10},{9,11},{10,... | collective-permute-start | bytes 1572872 | tf_op jit(solution)/shard_map/ppermute | solution.py:177
  113.1 64.1 %collective-permute-start.10 = (bf16[128,4096]{1,0:T(8,128)(2,1)S(1)}, bf16[128,4096]{1,0:T(8,128)(2,1)S(1)}, u32[]{:S(2)}, u32[]{:S(2)}) collective-permute-start(bf16[128,4096]{1,0:T(8,128)(2,1)S(1)} %copy-done.9), channel_id=1, source_target_pairs={{2,1},{1,0},{6,5},{5,4},{10,9},{9,8},{14,13},{13,12},{18,17},{17,1... | collective-permute-start | bytes 3145736 | tf_op jit(solution)/shard_map/ppermute | solution.py:185
  114.4 62.8 %collective-permute-start.11 = (bf16[128,4096]{1,0:T(8,128)(2,1)S(1)}, bf16[128,4096]{1,0:T(8,128)(2,1)S(1)}, u32[]{:S(2)}, u32[]{:S(2)}) collective-permute-start(bf16[128,4096]{1,0:T(8,128)(2,1)S(1)} %copy-done.7), channel_id=1, source_target_pairs={{1,2},{2,3},{5,6},{6,7},{9,10},{10,11},{13,14},{14,15},{17,18},{18... | collective-permute-start | bytes 3145736 | tf_op jit(solution)/shard_map/ppermute | solution.py:185
  177.2 59.6 %collective-permute-start.4 = (bf16[512,512]{1,0:T(8,128)(2,1)}, bf16[512,512]{1,0:T(8,128)(2,1)}, u32[]{:S(2)}, u32[]{:S(2)}) collective-permute-start(bf16[512,512]{1,0:T(8,128)(2,1)} %bitcast.2.refs_0_), channel_id=1, source_target_pairs={{0,3},{1,0},{2,1},{3,2},{4,7},{5,4},{6,5},{7,6},{8,11},{9,8},{10,9... | collective-permute-start | bytes 1572872 | tf_op jit(solution)/shard_map/ppermute | solution.py:177
  177.2 27.7 %collective-permute-start.13 = (bf16[128,512]{1,0:T(8,128)(2,1)S(1)}, bf16[128,512]{1,0:T(8,128)(2,1)S(1)}, u32[]{:S(2)}, u32[]{:S(2)}) collective-permute-start(bf16[128,512]{1,0:T(8,128)(2,1)S(1)} %get-tuple-element.18), channel_id=1, source_target_pairs={{0,1},{1,2},{2,3},{3,0},{4,5},{5,6},{6,7},{7,4},{8,9},{9,10},{10,1... | collective-permute-start | bytes 393224 | tf_op jit(solution)/shard_map/ppermute | solution.py:177
  224.9 55.2 %collective-permute-start.16 = (bf16[128,4096]{1,0:T(8,128)(2,1)}, bf16[128,4096]{1,0:T(8,128)(2,1)}, u32[]{:S(2)}, u32[]{:S(2)}) collective-permute-start(bf16[128,4096]{1,0:T(8,128)(2,1)} %get-tuple-element.13), channel_id=1, source_target_pairs={{0,1},{1,2},{2,3},{4,5},{5,6},{6,7},{8,9},{9,10},{10,11},{12,13},{... | collective-permute-start | bytes 3145736 | tf_op jit(solution)/shard_map/ppermute | solution.py:185
  230.0 48.7 %collective-permute-start.17 = (bf16[128,4096]{1,0:T(8,128)(2,1)}, bf16[128,4096]{1,0:T(8,128)(2,1)}, u32[]{:S(2)}, u32[]{:S(2)}) collective-permute-start(bf16[128,4096]{1,0:T(8,128)(2,1)} %get-tuple-element.13), channel_id=1, source_target_pairs={{1,0},{2,1},{3,2},{5,4},{6,5},{7,6},{9,8},{10,9},{11,10},{13,12},{... | collective-permute-start | bytes 3145736 | tf_op jit(solution)/shard_map/ppermute | solution.py:185
  231.3 73.2 %collective-permute-start.20 = (bf16[128,4096]{1,0:T(8,128)(2,1)}, bf16[128,4096]{1,0:T(8,128)(2,1)}, u32[]{:S(2)}, u32[]{:S(2)}) collective-permute-start(bf16[128,4096]{1,0:T(8,128)(2,1)} %get-tuple-element.13), channel_id=1, source_target_pairs={{0,3},{3,0},{4,7},{7,4},{8,11},{11,8},{12,15},{15,12},{16,19},{19,... | collective-permute-start | bytes 3145736 | tf_op jit(solution)/shard_map/ppermute | solution.py:185
  270.8 43.1 %all-to-all-start = ((bf16[8,2,32,1536]{3,2,1,0:T(8,128)(2,1)}), bf16[8,2,32,1536]{3,2,1,0:T(8,128)(2,1)S(1)}, u32[]{:S(2)}, u32[]{:S(2)}) async-start(bf16[8,2,32,1536]{3,2,1,0:T(8,128)(2,1)} %bitcast.77), calls=%async_computation | async-start | bytes 3145728 | tf_op jit(solution)/shard_map/all_to_all | solution.py:285
  278.7 25.5 %collective-permute-start.18 = (bf16[128,4096]{1,0:T(8,128)(2,1)}, bf16[128,4096]{1,0:T(8,128)(2,1)S(1)}, u32[]{:S(2)}, u32[]{:S(2)}) collective-permute-start(bf16[128,4096]{1,0:T(8,128)(2,1)} %collective-permute-done.17), channel_id=1, source_target_pairs={{2,1},{1,0},{6,5},{5,4},{10,9},{9,8},{14,13},{13,12},{18,17},{17,1... | collective-permute-start | bytes 3145736 | tf_op jit(solution)/shard_map/ppermute | solution.py:185
  280.1 24.0 %collective-permute-start.19 = (bf16[128,4096]{1,0:T(8,128)(2,1)}, bf16[128,4096]{1,0:T(8,128)(2,1)S(1)}, u32[]{:S(2)}, u32[]{:S(2)}) collective-permute-start(bf16[128,4096]{1,0:T(8,128)(2,1)} %collective-permute-done.16), channel_id=1, source_target_pairs={{1,2},{2,3},{5,6},{6,7},{9,10},{10,11},{13,14},{14,15},{17,18},{18... | collective-permute-start | bytes 3145736 | tf_op jit(solution)/shard_map/ppermute | solution.py:185
  314.0 24.5 %all-to-all-start.2 = ((bf16[8,2,32,1536]{3,2,1,0:T(8,128)(2,1)}), bf16[8,2,32,1536]{3,2,1,0:T(8,128)(2,1)S(1)}, u32[]{:S(2)}, u32[]{:S(2)}) async-start(bf16[8,2,32,1536]{3,2,1,0:T(8,128)(2,1)} %bitcast.86), calls=%async_computation.2 | async-start | bytes 3145728 | tf_op jit(solution)/shard_map/all_to_all | solution.py:285
  (20 other events, 139.0 us)
Sparse Core Ops, SparseCore 0:
  9.9 42.0 all-gather.7
  100.6 69.3 all-gather.9
  172.0 74.5 all-gather.5
